TPU v7x, 128 devices: a whole 4x4x4 slice. The times are simulated.
128 devices in a mesh: prefix: 16 (over z, x_hi, core), resp: 8 (over y, x_lo).
Axes of the slice: x: 4 (x_hi: 2, x_lo: 2; x = x_hi * 2 + x_lo), y: 4, z: 4, core: 2. Of those that a mesh axis runs over, the one named last changes fastest.
Arguments:
- resp_query: bfloat16 [16, 1024, 5120], P('prefix', 'resp'), may hold values from -120 to 120
- resp_keys: bfloat16 [16, 1024, 1024], P('prefix', 'resp'), may hold values from -5 to 5
- resp_values: bfloat16 [16, 1024, 1024], P('prefix', 'resp'), may hold values from -5 to 5
- resp_out: bfloat16 [16, 1024, 5120], P('prefix', 'resp'), may hold values from -6 to 6
- resp_grad: bfloat16 [16, 1024, 5120], P('prefix', 'resp'), may hold values from -24 to 24
- prompt_keys: bfloat16 [1024, 1024], P('prefix'), may hold values from -4 to 4
- prompt_values: bfloat16 [1024, 1024], P('prefix'), may hold values from -5 to 5
- resp_lengths: int32 [16], P('prefix'), may hold values from 1 to 1024, 10240 in all
Outputs:
- grad_query: bfloat16 [16, 1024, 5120], P('prefix', 'resp')
- grad_resp_keys: bfloat16 [16, 1024, 1024], P('prefix', 'resp')
- grad_resp_values: bfloat16 [16, 1024, 1024], P('prefix', 'resp')
- grad_prompt_keys: bfloat16 [1024, 1024], P(('prefix', 'resp'))
- grad_prompt_values: bfloat16 [1024, 1024], P(('prefix', 'resp'))
Inputs may be any that keep to these rules, and one draw needn't show every extreme that they name: `resp_lengths`: one response fills all 1024 slots.
All inputs are finite; a program needn't handle non-finite values. No bound on the sum of `resp_lengths` on one device may be relied on, other than what follows from the above.
Results may differ from a plain program's by a relative error of at most 0.019.
Values may be sent and summed in bfloat16 or wider, within the bound.
No kernel may reach another device: no remote copies, remote signals or barrier semaphores. Data moves between devices by JAX's collectives and lax.ppermute only.
A program may use at most 192 MiB of HBM per device.

v0:
```python
import jax
import jax.numpy as jnp
from jax import lax
from jax.experimental import pallas as pl
from jax.experimental.pallas import tpu as pltpu
from jax.sharding import PartitionSpec as P

HEADS = 40
KV_HEADS = 8
GROUP = HEADS // KV_HEADS
HEAD_DIM = 128
SCALE = HEAD_DIM ** (-0.5)
EXP2_SCALE = SCALE * 1.4426950408889634
QW = GROUP * HEAD_DIM
TILE = 256
STATS = 16
UNSEEN = -1e30
PACK_ROWS = 32
GATHER_BITS = (1, 0, 2, 3)
COLUMNS = 2 + 2 * GROUP
DELTA_ROWS = 16
BACK_W = QW + 2 * HEAD_DIM
X_BIT, CORE_BIT = 2, 1

NN = (((1,), (0,)), ((), ()))
BF16 = jnp.bfloat16
F32 = jnp.float32
ANY = pl.BlockSpec(memory_space=pl.ANY)
HBM = pl.BlockSpec(memory_space=pltpu.HBM)
VMEM = pl.BlockSpec(memory_space=pltpu.VMEM)
SMEM = pl.BlockSpec(memory_space=pltpu.SMEM)


def dot(a, b, dims):
    return lax.dot_general(a, b, dims, preferred_element_type=F32)


def params(mib):
    return pltpu.CompilerParams(vmem_limit_bytes=mib * 1024 * 1024)


def times(index, size):
    return pl.multiple_of(index * size, size)


def send_rows(c, n):
    first = (c * COLUMNS + n) * PACK_ROWS
    return slice(first, first + PACK_ROWS)


def gather_mask(index):
    return sum(((index >> step) & 1) << bit for step, bit in enumerate(GATHER_BITS))


def start_all(copies, sems):
    started = [pltpu.make_async_copy(src, dst, sems.at[n]) for n, (src, dst) in enumerate(copies)]
    for copy in started:
        copy.start()
    return started


def pack_kernel(q_in, g_in, o_in, k_in, v_in, send_out, q_ref, g_ref, o_ref, k_ref, v_ref, send_ref, left_ref, sems, out_sems):
    ins = ((q_in, q_ref), (g_in, g_ref), (o_in, o_ref), (k_in, k_ref), (v_in, v_ref))
    steps = q_ref.shape[0] // PACK_ROWS
    arriving = []
    for c in range(steps):
        rows = slice(c * PACK_ROWS, (c + 1) * PACK_ROWS)
        arriving.append(start_all([(src.at[rows], dst.at[rows]) for src, dst in ins], sems.at[c]))
    row = lax.broadcasted_iota(jnp.int32, (QW, HEAD_DIM), 0) // HEAD_DIM
    lane = lax.broadcasted_iota(jnp.int32, (QW, HEAD_DIM), 1)
    ones = jnp.where((lane >= 3 * row) & (lane < 3 * row + 3), 1.0, 0.0).astype(BF16)
    leaving = []
    for c in range(steps):
        rows = slice(c * PACK_ROWS, (c + 1) * PACK_ROWS)
        for copy in arriving[c]:
            copy.wait()
        highs, lows = [], []
        for h in range(KV_HEADS):
            columns = [(k_ref, h), (v_ref, h)]
            columns += [(q_ref, h * GROUP + j) for j in range(GROUP)]
            columns += [(g_ref, h * GROUP + j) for j in range(GROUP)]
            for n, (ref, col) in enumerate(columns):
                send_ref[h, send_rows(c, n)] = ref[rows, col * HEAD_DIM : (col + 1) * HEAD_DIM]
            wide = slice(h * QW, (h + 1) * QW)
            product = g_ref[rows, wide].astype(F32) * o_ref[rows, wide].astype(F32)
            high = product.astype(BF16)
            highs.append(high)
            lows.append((product - high.astype(F32)).astype(BF16))
        part = slice(c * COLUMNS * PACK_ROWS, (c + 1) * COLUMNS * PACK_ROWS)
        leaving += start_all([(send_ref.at[:, part], send_out.at[:, part])], out_sems.at[pl.ds(c, 1)])
        left = dot(jnp.concatenate(highs), ones, NN) + dot(jnp.concatenate(lows), ones, NN)
        for h in range(KV_HEADS):
            left_ref[h, rows] = left[h * PACK_ROWS : (h + 1) * PACK_ROWS]
    part = lax.broadcasted_iota(jnp.int32, (DELTA_ROWS, q_ref.shape[0]), 0) % 3
    last = slice(steps * COLUMNS * PACK_ROWS, steps * COLUMNS * PACK_ROWS + DELTA_ROWS)
    for h in range(KV_HEADS):
        left = left_ref[h].T[0:DELTA_ROWS]
        first = left.astype(BF16).astype(F32)
        second = (left - first).astype(BF16).astype(F32)
        third = left - first - second
        send_ref[h, last] = jnp.where(part == 0, first, jnp.where(part == 1, second, third)).astype(BF16)
    leaving += start_all([(send_ref.at[:, last], send_out.at[:, last])], out_sems.at[pl.ds(steps, 1)])
    for copy in leaving:
        copy.wait()


def pack(q, g, o, k, v):
    rows = q.shape[0]
    steps = rows // PACK_ROWS
    send = (KV_HEADS, rows * COLUMNS + DELTA_ROWS, HEAD_DIM)
    return pl.pallas_call(
        pack_kernel,
        in_specs=[HBM] * 5,
        out_specs=HBM,
        out_shape=pltpu.HBM(send, BF16),
        scratch_shapes=[pltpu.VMEM(a.shape, BF16) for a in (q, g, o, k, v)]
        + [
            pltpu.VMEM(send, BF16),
            pltpu.VMEM((KV_HEADS, rows, HEAD_DIM), F32),
            pltpu.SemaphoreType.DMA((steps, 5)),
            pltpu.SemaphoreType.DMA((steps + 1,)),
        ],
        compiler_params=params(60),
        name="pack",
    )(q, g, o, k, v)


def unpack_kernel(back_ref, q_ref, k_ref, v_ref, sems):
    copies = []
    for h in range(KV_HEADS):
        thin = slice(h * HEAD_DIM, (h + 1) * HEAD_DIM)
        wide = slice(h * QW, (h + 1) * QW)
        copies.append((back_ref.at[h, :, 0:QW], q_ref.at[:, wide]))
        copies.append((back_ref.at[h, :, QW : QW + HEAD_DIM], k_ref.at[:, thin]))
        copies.append((back_ref.at[h, :, QW + HEAD_DIM :], v_ref.at[:, thin]))
    for copy in start_all(copies, sems):
        copy.wait()


def unpack(back):
    rows = back.shape[1]
    return pl.pallas_call(
        unpack_kernel,
        in_specs=[ANY],
        out_specs=[ANY] * 3,
        out_shape=[
            jax.ShapeDtypeStruct((rows, KV_HEADS * QW), BF16),
            jax.ShapeDtypeStruct((rows, KV_HEADS * HEAD_DIM), BF16),
            jax.ShapeDtypeStruct((rows, KV_HEADS * HEAD_DIM), BF16),
        ],
        scratch_shapes=[pltpu.SemaphoreType.DMA((3 * KV_HEADS,))],
        compiler_params=params(4),
        name="unpack",
    )(back)


def attend_kernel(place_ref, x_ref, pkv_low, pkv_high, back_out, pg_keep, pg_give, *refs):
    pkv_ref, back_ref, pg_ref, sems, block_sems, k_all, v_all, k_t = refs[:8]
    p_s, l_s, dq_t, dk, dv = refs[8:13]
    sets = [refs[13:20], refs[20:27]]
    prompt = pkv_ref.shape[0]
    run = (x_ref.shape[1] - DELTA_ROWS) // COLUMNS
    slots = KV_HEADS * run
    wide = GROUP * TILE
    prompt_tiles = prompt // TILE
    length, me_prefix = place_ref[0], place_ref[1]
    half = pkv_low.shape[0]
    sources = 2 * half
    share = prompt // sources
    copies = [
        ((pkv_low, pkv_high)[f // half].at[f % half], pkv_ref.at[pl.ds(times(me_prefix ^ gather_mask(f), share), share)])
        for f in range(sources)
    ]
    copies = start_all(copies, sems)
    back_ref[...] = jnp.zeros_like(back_ref)
    dk[...] = jnp.zeros_like(dk)
    dv[...] = jnp.zeros_like(dv)
    for block in sets:
        block[3][HEAD_DIM + DELTA_ROWS :] = jnp.zeros((HEAD_DIM - DELTA_ROWS, wide), BF16)
    for copy in copies:
        copy.wait()

    def flip(a):
        return a.astype(F32).T.astype(BF16)

    def slots_of(b, n):
        return jnp.concatenate([x_ref[b, send_rows(c, n)] for c in range(run // PACK_ROWS)])

    k_all[0:prompt] = pkv_ref[:, 0:HEAD_DIM]
    v_all[0:prompt, 0:HEAD_DIM] = pkv_ref[:, HEAD_DIM:]
    for b in range(KV_HEADS):
        own = slice(prompt + b * run, prompt + (b + 1) * run)
        k_all[own] = slots_of(b, 0)
        v_all[own, 0:HEAD_DIM] = slots_of(b, 1)
    v_all[:, HEAD_DIM:] = jnp.full((prompt + slots, HEAD_DIM), -1.0, BF16)
    for t in range((prompt + slots) // TILE):
        block = slice(t * TILE, (t + 1) * TILE)
        k_t[:, block] = flip(k_all[block])

    def lanes(j):
        return slice(j * TILE, (j + 1) * TILE)

    def tile_rows(t, count):
        return pl.ds(times(t, TILE), count * TILE)

    def stat_rows(t, count):
        return pl.ds(times(t, STATS), count * STATS)

    def sweep(body, tiles):
        def pair(n, carry):
            body(2 * n, 2)
            return carry

        last = 2 - tiles % 2
        lax.fori_loop(0, (tiles - last) // 2, pair, 0)
        body(tiles - last, last)

    def load_block(i, block):
        qs, gs, qs_t, gs_t = block[:4]
        sources = range(i * TILE // run, (i + 1) * TILE // run)
        delta_t = jnp.concatenate([x_ref[b, run * COLUMNS :] for b in sources], axis=1).astype(F32)
        part = lax.broadcasted_iota(jnp.int32, delta_t.shape, 0)
        for j in range(GROUP):
            q = jnp.concatenate([slots_of(b, 2 + j) for b in sources])
            g = jnp.concatenate([slots_of(b, 2 + GROUP + j) for b in sources])
            qs[lanes(j)] = q
            gs[lanes(j)] = g
            qs_t[:, lanes(j)] = flip(q)
            gs_t[0:HEAD_DIM, lanes(j)] = flip(g)
            mine = (part >= 3 * j) & (part < 3 * j + 3)
            gs_t[HEAD_DIM : HEAD_DIM + DELTA_ROWS, lanes(j)] = jnp.where(mine, delta_t, 0.0).astype(BF16)

    def score_head(t, count, j, block, diagonal=False):
        qs_t, _, e_all, tops, sums = block[2:]
        s = dot(k_all[tile_rows(t, count)], qs_t[:, lanes(j)], NN)
        if diagonal:
            seen = lax.broadcasted_iota(jnp.int32, s.shape, 0) <= lax.broadcasted_iota(
                jnp.int32, s.shape, 1
            )
            s = jnp.where(seen, s, UNSEEN)
        groups = count * STATS // 8
        s = s.reshape(groups, -1, 8, TILE)
        top = jnp.max(s, axis=1, keepdims=True)
        e = jnp.exp2((s - top) * EXP2_SCALE)
        tops[stat_rows(t, count), lanes(j)] = top.reshape(groups * 8, TILE)
        sums[stat_rows(t, count), lanes(j)] = jnp.sum(e, axis=1).reshape(groups * 8, TILE)
        e_all[tile_rows(t, count), lanes(j)] = e.reshape(count * TILE, TILE)

    def normalise(i, block):
        tops, sums = block[5:]
        rows = STATS * (prompt_tiles + i + 1)
        top = tops[0:rows]
        weight = jnp.exp2((top - jnp.max(top, axis=0, keepdims=True)) * EXP2_SCALE)
        total = jnp.sum(weight * sums[0:rows], axis=0, keepdims=True)
        slot = lax.broadcasted_iota(jnp.int32, (1, wide), 1) % TILE + i * TILE
        tops[0:rows] = weight * (jnp.where(slot < length, 1.0, 0.0) / total)

    def grad_head(t, count, j, block):
        gs_t, e_all, factors = block[3:6]
        shifted = dot(v_all[tile_rows(t, count)], gs_t[:, lanes(j)], NN)
        groups = count * STATS // 8
        e = e_all[tile_rows(t, count), lanes(j)].reshape(groups, -1, 8, TILE)
        factor = factors[stat_rows(t, count), lanes(j)].reshape(groups, 1, 8, TILE)
        p = (e * factor).reshape(count * TILE, TILE)
        p_s[0 : count * TILE, lanes(j)] = p.astype(BF16)
        l_s[0 : count * TILE, lanes(j)] = (p * shifted).astype(BF16)

    def grad_sums(t, count, block):
        qs, gs = block[:2]
        keys, held = tile_rows(t, count), slice(0, count * TILE)
        dv[keys] += dot(p_s[held], gs[...], NN)
        dk[keys] += dot(l_s[held], qs[...], NN)
        dq_t[...] += dot(k_t[:, keys], l_s[held], NN)

    def leaving(i):
        part = (slice(i * TILE, (i + 1) * TILE), slice(0, QW))
        return pltpu.make_async_copy(back_ref.at[part], back_out.at[part], block_sems.at[i])

    def finish(i):
        here = slice(i * TILE, (i + 1) * TILE)
        for j in range(GROUP):
            back_ref[here, j * HEAD_DIM : (j + 1) * HEAD_DIM] = (
                (dq_t[:, lanes(j)] * SCALE).T.astype(BF16)
            )
        leaving(i).start()

    def scores(t, count):
        for j in range(GROUP):
            score_head(t, count, j, sets[0])

    load_block(0, sets[0])
    sweep(scores, prompt_tiles)
    for j in range(GROUP):
        score_head(prompt_tiles, 1, j, sets[0], diagonal=True)
    normalise(0, sets[0])
    load_block(1, sets[1])

    blocks = slots // TILE
    live = lax.div(length + TILE - 1, TILE)
    for i in range(blocks):
        now, later = sets[i % 2], sets[(i + 1) % 2]
        tiles = prompt_tiles + i + 1
        dq_t[...] = jnp.zeros_like(dq_t)

        def grads(t, count):
            for j in range(GROUP):
                grad_head(t, count, j, now)
            grad_sums(t, count, now)

        def both(t, count):
            for j in range(GROUP):
                grad_head(t, count, j, now)
                score_head(t, count, j, later)
            grad_sums(t, count, now)

        if i + 1 < blocks:

            @pl.when(live > i + 1)
            def _():
                sweep(both, tiles)
                for j in range(GROUP):
                    score_head(tiles, 1, j, later, diagonal=True)
                finish(i)
                normalise(i + 1, later)
                if i + 2 < blocks:
                    load_block(i + 2, now)

        @pl.when(live == i + 1)
        def _():
            sweep(grads, tiles)
            finish(i)

        @pl.when(live <= i)
        def _():
            leaving(i).start()

    pg_ref[:, 0:HEAD_DIM] = (dk[0:prompt] * SCALE).astype(BF16)
    pg_ref[:, HEAD_DIM:] = dv[0:prompt].astype(BF16)
    back_ref[:, QW : QW + HEAD_DIM] = (dk[prompt:] * SCALE).astype(BF16)
    back_ref[:, QW + HEAD_DIM :] = dv[prompt:].astype(BF16)
    mine = me_prefix & X_BIT
    copies = [
        (pg_ref.at[pl.ds(times(f + (f & -X_BIT) + (mine ^ bit), share), share)], out.at[f])
        for bit, out in ((0, pg_keep), (X_BIT, pg_give))
        for f in range(half)
    ]
    copies = start_all([(back_ref.at[:, QW:], back_out.at[:, QW:])] + copies, sems)
    for i in range(blocks):
        leaving(i).wait()
    for copy in copies:
        copy.wait()


def attend(place, x, pkv):
    slots = KV_HEADS * (x.shape[1] - DELTA_ROWS) // COLUMNS
    half, share, prompt_width = pkv[0].shape
    responses = 2 * half
    prompt = responses * share
    keys = slots + prompt
    wide = GROUP * TILE
    outs = [((slots, BACK_W), BF16)] + [((half, share, prompt_width), BF16)] * 2
    stats = pltpu.VMEM((keys // TILE * STATS, wide), F32)
    one_set = [
        pltpu.VMEM((wide, HEAD_DIM), BF16),
        pltpu.VMEM((wide, HEAD_DIM), BF16),
        pltpu.VMEM((HEAD_DIM, wide), BF16),
        pltpu.VMEM((2 * HEAD_DIM, wide), BF16),
        pltpu.VMEM((keys, wide), F32),
        stats,
        stats,
    ]
    return pl.pallas_call(
        attend_kernel,
        in_specs=[SMEM, VMEM, ANY, ANY],
        out_specs=[HBM] * len(outs),
        out_shape=[pltpu.HBM(shape, dtype) for shape, dtype in outs],
        scratch_shapes=[
            pltpu.VMEM((prompt, prompt_width), BF16),
            pltpu.VMEM((slots, BACK_W), BF16),
            pltpu.VMEM((prompt, prompt_width), BF16),
            pltpu.SemaphoreType.DMA((1 + responses,)),
            pltpu.SemaphoreType.DMA((slots // TILE,)),
            pltpu.VMEM((keys, HEAD_DIM), BF16),
            pltpu.VMEM((keys, 2 * HEAD_DIM), BF16),
            pltpu.VMEM((HEAD_DIM, keys), BF16),
            pltpu.VMEM((2 * TILE, wide), BF16),
            pltpu.VMEM((2 * TILE, wide), BF16),
            pltpu.VMEM((HEAD_DIM, wide), F32),
            pltpu.VMEM((keys, HEAD_DIM), F32),
            pltpu.VMEM((keys, HEAD_DIM), F32),
        ]
        + one_set * 2,
        compiler_params=params(50),
        cost_estimate=pl.CostEstimate(
            flops=10 * slots * keys * QW, transcendentals=0, bytes_accessed=8 * slots * QW
        ),
        name="attend",
    )(place, pltpu.with_memory_space_constraint(x, pltpu.VMEM), *pkv)


def core_kernel(place_ref, mine_ref, got_ref, keep_ref, give_ref, total):
    total[...] = mine_ref[...].astype(F32) + got_ref[...].astype(F32)
    core = place_ref[1] & CORE_BIT
    for f in range(keep_ref.shape[0]):
        keep_ref[f] = total[2 * f + core]
        give_ref[f] = total[2 * f + 1 - core]


def sum_over_x(place, mine, got):
    count, share, width = mine.shape
    part = jax.ShapeDtypeStruct((count // 2, share, width), F32)
    return pl.pallas_call(
        core_kernel,
        in_specs=[SMEM, VMEM, VMEM],
        out_specs=[VMEM] * 2,
        out_shape=[part] * 2,
        scratch_shapes=[pltpu.VMEM(mine.shape, F32)],
        compiler_params=params(8),
        cost_estimate=pl.CostEstimate(flops=5 * 10**10, transcendentals=0, bytes_accessed=2**20),
        name="sum_over_x",
    )(place, mine, got)


def z_kernel(place_ref, mine_ref, got_ref, *refs):
    outs, total = refs[:-1], refs[-1]
    total[...] = mine_ref[...] + got_ref[...]
    z = place_ref[1] // (2 * X_BIT)
    for d, out in enumerate(outs):
        out[...] = total[z ^ d]


def sum_over_cores(place, mine, got):
    count, share, width = mine.shape
    return pl.pallas_call(
        z_kernel,
        in_specs=[SMEM, VMEM, VMEM],
        out_specs=[VMEM] * count,
        out_shape=[jax.ShapeDtypeStruct((share, width), F32)] * count,
        scratch_shapes=[pltpu.VMEM(mine.shape, F32)],
        compiler_params=params(8),
        name="sum_over_cores",
    )(place, mine, got)


def sum_kernel(place_ref, *refs):
    parts, outs, total = refs[: -KV_HEADS - 1], refs[-KV_HEADS - 1 : -1], refs[-1]
    value = parts[0][...]
    for part in parts[1:]:
        value = value + part[...]
    total[...] = value
    own = outs[0].shape[0]
    for d, out in enumerate(outs):
        out[...] = total[pl.ds(times(place_ref[2] ^ d, own), own)]


def sum_parts(place, parts):
    rows, width = parts[0].shape
    own = rows // KV_HEADS
    return pl.pallas_call(
        sum_kernel,
        in_specs=[SMEM] + [VMEM] * len(parts),
        out_specs=[VMEM] * KV_HEADS,
        out_shape=[jax.ShapeDtypeStruct((own, width), F32)] * KV_HEADS,
        scratch_shapes=[pltpu.VMEM((rows, width), F32)],
        compiler_params=params(4),
        name="sum_parts",
    )(place, *parts)


def spread_kernel(place_ref, *refs):
    parts, (k_ref, v_ref) = refs[:KV_HEADS], refs[KV_HEADS:]
    for d, part in enumerate(parts):
        cols = pl.ds(times(place_ref[2] ^ d, HEAD_DIM), HEAD_DIM)
        k_ref[:, cols] = part[:, 0:HEAD_DIM].astype(BF16)
        v_ref[:, cols] = part[:, HEAD_DIM:].astype(BF16)


def spread_heads(place, parts):
    shape = jax.ShapeDtypeStruct((parts[0].shape[0], KV_HEADS * HEAD_DIM), BF16)
    return pl.pallas_call(
        spread_kernel,
        in_specs=[SMEM] + [VMEM] * KV_HEADS,
        out_specs=[VMEM] * 2,
        out_shape=[shape] * 2,
        compiler_params=params(4),
        name="spread_heads",
    )(place, *parts)


def swap(value, axis, d):
    return lax.ppermute(value, axis, [(i, i ^ d) for i in range(lax.axis_size(axis))])


def swap_all(values, axis, step=1):
    return [values[0]] + [swap(values[d], axis, step * d) for d in range(1, len(values))]


def swap_across(value):
    sizes = lax.axis_size("prefix"), lax.axis_size("resp")
    pairs = [(p * sizes[1] + r, (p ^ X_BIT) * sizes[1] + (r ^ 1)) for p in range(sizes[0]) for r in range(sizes[1])]
    return lax.ppermute(value, ("prefix", "resp"), pairs)


def local(
    resp_query,
    resp_keys,
    resp_values,
    resp_out,
    resp_grad,
    prompt_keys,
    prompt_values,
    resp_lengths,
):
    head = lax.axis_index("resp")
    rows = resp_query.shape[1]
    place = jnp.stack([resp_lengths[0], lax.axis_index("prefix"), head])
    send = pack(resp_query[0], resp_grad[0], resp_out[0], resp_keys[0], resp_values[0])
    x = lax.all_to_all(send, "resp", 0, 0, tiled=True)
    prompt_keys, prompt_values, _ = lax.optimization_barrier((prompt_keys, prompt_values, send))
    cut = lambda a, h: lax.dynamic_slice_in_dim(a, h * HEAD_DIM, HEAD_DIM, 1)
    both = lambda h: jnp.concatenate([cut(prompt_keys, h), cut(prompt_values, h)], axis=1)[None]
    pkv, first = both(head), swap_across(both(head ^ 1))
    pkv = jnp.concatenate([pkv, first])
    for bit in GATHER_BITS[1:-1]:
        pkv = jnp.concatenate([pkv, swap(pkv, "prefix", 1 << bit)])
    pkv = [pkv, swap(pkv, "prefix", 1 << GATHER_BITS[-1])]
    back, keep, give = attend(place, x, pkv)
    back = lax.all_to_all(back.reshape(KV_HEADS, rows, BACK_W), "resp", 0, 0, tiled=True)
    keep, give = sum_over_x(place, keep, swap(give, "prefix", X_BIT))
    parts = sum_over_cores(place, keep, swap(give, "prefix", CORE_BIT))
    parts = swap_all(sum_parts(place, swap_all(parts, "prefix", 2 * X_BIT)), "resp")
    total = spread_heads(place, parts)
    grad_query, grad_keys, grad_values = unpack(back)
    return (grad_query[None], grad_keys[None], grad_values[None], total[0], total[1])


def solution(mesh):
    return jax.shard_map(
        local,
        mesh=mesh,
        in_specs=(
            P("prefix", "resp", None),
            P("prefix", "resp", None),
            P("prefix", "resp", None),
            P("prefix", "resp", None),
            P("prefix", "resp", None),
            P("prefix", None),
            P("prefix", None),
            P("prefix"),
        ),
        out_specs=(
            P("prefix", "resp", None),
            P("prefix", "resp", None),
            P("prefix", "resp", None),
            P(("prefix", "resp"), None),
            P(("prefix", "resp"), None),
        ),
        check_vma=False,
    )
```

profile of v0, /device:TPU:0, one launch (start us, length us, event | category | flops | bytes accessed | tf_op | source)
XLA Modules:
  0.0 119.6 jit_solution(5951985595096808009)
XLA Ops:
  0.6 4.2 %pack.1 = bf16[8,1552,128]{2,1,0:T(8,128)(2,1)} custom-call(bf16[128,5120]{1,0:T(8,128)(2,1)} %bitcast.16, bf16[128,5120]{1,0:T(8,128)(2,1)} %bitcast.17, bf16[128,5120]{1,0:T(8,128)(2,1)} %bitcast.18, bf16[128,1024]{1,0:T(8,128)(2,1)} %bitcast.19, bf16[128,1024]{1,0:T(8,128)(2,1)} %bitcast.20), custom_call_target="tpu_custom_call" | custom-call | tf_op jit(solution)/shard_map/pack/pallas_call | solution.py:111
  4.9 5.5 %all-to-all-start = ((bf16[8,1552,128]{2,1,0:T(8,128)(2,1)}), bf16[8,1552,128]{2,1,0:T(8,128)(2,1)S(1)}, u32[]{:S(2)}, u32[]{:S(2)}) async-start(bf16[8,1552,128]{2,1,0:T(8,128)(2,1)} %pack.1), calls=%async_computation | async-start | bytes 6356992 | tf_op jit(solution)/shard_map/all_to_all | solution.py:518
  11.2 3.4 %collective-permute-start = (bf16[1,64,256]{2,1,0:T(8,128)(2,1)S(1)}, bf16[1,64,256]{2,1,0:T(8,128)(2,1)S(1)}, u32[]{:S(2)}, u32[]{:S(2)}) collective-permute-start(bf16[1,64,256]{2,1,0:T(8,128)(2,1)S(1)} %maximum_bitcast_fusion.1), channel_id=1, source_target_pairs={{0,17},{1,16},{2,19},{3,18},{4,21},{5,20},{6,23},{7,22},{8,25},{9,... | collective-permute-start | bytes 98312 | tf_op jit(solution)/shard_map/ppermute | solution.py:501
  14.5 1.9 %collective-permute-done = bf16[1,64,256]{2,1,0:T(8,128)(2,1)S(1)} collective-permute-done((bf16[1,64,256]{2,1,0:T(8,128)(2,1)S(1)}, bf16[1,64,256]{2,1,0:T(8,128)(2,1)S(1)}, u32[]{:S(2)}, u32[]{:S(2)}) %collective-permute-start) | collective-permute-done | bytes 32800 | tf_op jit(solution)/shard_map/ppermute | solution.py:501
  16.5 1.2 %collective-permute-done.1 = bf16[2,64,256]{2,1,0:T(8,128)(2,1)S(1)} collective-permute-done((bf16[2,64,256]{2,1,0:T(8,128)(2,1)S(1)}, bf16[2,64,256]{2,1,0:T(8,128)(2,1)S(1)}, u32[]{:S(2)}, u32[]{:S(2)}) %collective-permute-start.1) | collective-permute-done | bytes 65568 | tf_op jit(solution)/shard_map/ppermute | solution.py:491
  17.8 2.0 %collective-permute-start.2 = (bf16[4,64,256]{2,1,0:T(8,128)(2,1)S(1)}, bf16[4,64,256]{2,1,0:T(8,128)(2,1)S(1)}, u32[]{:S(2)}, u32[]{:S(2)}) collective-permute-start(bf16[4,64,256]{2,1,0:T(8,128)(2,1)S(1)} %pad_maximum_fusion.1), channel_id=1, source_target_pairs={{0,32},{8,40},{16,48},{24,56},{32,0},{40,8},{48,16},{56,24},{64,96... | collective-permute-start | bytes 393224 | tf_op jit(solution)/shard_map/ppermute | solution.py:491
  19.8 3.8 %collective-permute-done.2 = bf16[4,64,256]{2,1,0:T(8,128)(2,1)S(1)} collective-permute-done((bf16[4,64,256]{2,1,0:T(8,128)(2,1)S(1)}, bf16[4,64,256]{2,1,0:T(8,128)(2,1)S(1)}, u32[]{:S(2)}, u32[]{:S(2)}) %collective-permute-start.2) | collective-permute-done | bytes 131104 | tf_op jit(solution)/shard_map/ppermute | solution.py:491
  23.6 3.8 %collective-permute-start.3 = (bf16[8,64,256]{2,1,0:T(8,128)(2,1)S(1)}, bf16[8,64,256]{2,1,0:T(8,128)(2,1)}, u32[]{:S(2)}, u32[]{:S(2)}) collective-permute-start(bf16[8,64,256]{2,1,0:T(8,128)(2,1)S(1)} %pad_maximum_fusion.pkv_low), channel_id=1, source_target_pairs={{0,64},{8,72},{16,80},{24,88},{32,96},{40,104},{48,112},{56,120},{... | collective-permute-start | bytes 786440 | tf_op jit(solution)/shard_map/ppermute | solution.py:491
  28.2 5.2 %collective-permute-done.3.pkv_high = bf16[8,64,256]{2,1,0:T(8,128)(2,1)} collective-permute-done((bf16[8,64,256]{2,1,0:T(8,128)(2,1)S(1)}, bf16[8,64,256]{2,1,0:T(8,128)(2,1)}, u32[]{:S(2)}, u32[]{:S(2)}) %collective-permute-start.3) | collective-permute-done | bytes 262176 | tf_op jit(solution)/shard_map/ppermute | solution.py:491
  33.3 15.6 %all-to-all-done.x_ref = bf16[8,1552,128]{2,1,0:T(8,128)(2,1)S(1)} async-done(((bf16[8,1552,128]{2,1,0:T(8,128)(2,1)}), bf16[8,1552,128]{2,1,0:T(8,128)(2,1)S(1)}, u32[]{:S(2)}, u32[]{:S(2)}) %all-to-all-start) | async-done | bytes 3178528 | tf_op jit(solution)/shard_map/all_to_all | solution.py:518
  48.9 22.0 %attend.1 = (bf16[1024,896]{1,0:T(8,128)(2,1)}, bf16[8,64,256]{2,1,0:T(8,128)(2,1)}, bf16[8,64,256]{2,1,0:T(8,128)(2,1)}) custom-call(s32[3]{0:T(128)S(1)} %pad_add_fusion.place_ref, bf16[8,1552,128]{2,1,0:T(8,128)(2,1)S(1)} %all-to-all-done.x_ref, bf16[8,64,256]{2,1,0:T(8,128)(2,1)S(1)} %pad_maximum_fusion.pkv_low, ...), custom_call_target="tpu_custom_call" | custom-call | flops 13421772800 | bytes 5242880 | tf_op jit(solution)/shard_map/attend/pallas_call | solution.py:372
  71.1 3.7 %all-to-all-start.1 = ((bf16[8,128,896]{2,1,0:T(8,128)(2,1)}), bf16[8,128,896]{2,1,0:T(8,128)(2,1)S(1)}, u32[]{:S(2)}, u32[]{:S(2)}) async-start(bf16[8,128,896]{2,1,0:T(8,128)(2,1)} %bitcast.15), calls=%async_computation.1 | async-start | bytes 3670016 | tf_op jit(solution)/shard_map/all_to_all | solution.py:528
  74.8 5.8 %collective-permute-done.4.got_ref = bf16[8,64,256]{2,1,0:T(8,128)(2,1)S(1)} collective-permute-done((bf16[8,64,256]{2,1,0:T(8,128)(2,1)}, bf16[8,64,256]{2,1,0:T(8,128)(2,1)S(1)}, u32[]{:S(2)}, u32[]{:S(2)}) %collective-permute-start.4) | collective-permute-done | bytes 262176 | tf_op jit(solution)/shard_map/ppermute | solution.py:491
  81.4 1.5 %collective-permute-done.5.got_ref = f32[4,64,256]{2,1,0:T(8,128)S(1)} collective-permute-done((f32[4,64,256]{2,1,0:T(8,128)S(1)}, f32[4,64,256]{2,1,0:T(8,128)S(1)}, u32[]{:S(2)}, u32[]{:S(2)}) %collective-permute-start.5) | collective-permute-done | bytes 262176 | tf_op jit(solution)/shard_map/ppermute | solution.py:491
  83.5 9.4 %collective-permute-start.6 = (f32[64,256]{1,0:T(8,128)S(1)}, f32[64,256]{1,0:T(8,128)S(1)}, u32[]{:S(2)}, u32[]{:S(2)}) collective-permute-start(f32[64,256]{1,0:T(8,128)S(1)} %get-tuple-element.40), channel_id=1, source_target_pairs={{0,32},{8,40},{16,48},{24,56},{32,0},{40,8},{48,16},{56,24},{64,96... | collective-permute-start | bytes 196616 | tf_op jit(solution)/shard_map/ppermute | solution.py:491
  92.9 2.3 %collective-permute-start.7 = (f32[64,256]{1,0:T(8,128)S(1)}, f32[64,256]{1,0:T(8,128)S(1)}, u32[]{:S(2)}, u32[]{:S(2)}) collective-permute-start(f32[64,256]{1,0:T(8,128)S(1)} %get-tuple-element.41), channel_id=1, source_target_pairs={{0,64},{8,72},{16,80},{24,88},{32,96},{40,104},{48,112},{56,120},{... | collective-permute-start | bytes 196616 | tf_op jit(solution)/shard_map/ppermute | solution.py:491
  95.7 3.3 %collective-permute-done.7.refs_2_ = f32[64,256]{1,0:T(8,128)S(1)} collective-permute-done((f32[64,256]{1,0:T(8,128)S(1)}, f32[64,256]{1,0:T(8,128)S(1)}, u32[]{:S(2)}, u32[]{:S(2)}) %collective-permute-start.7) | collective-permute-done | bytes 65568 | tf_op jit(solution)/shard_map/ppermute | solution.py:491
  99.0 1.7 %collective-permute-done.8.refs_3_ = f32[64,256]{1,0:T(8,128)S(1)} collective-permute-done((f32[64,256]{1,0:T(8,128)S(1)}, f32[64,256]{1,0:T(8,128)S(1)}, u32[]{:S(2)}, u32[]{:S(2)}) %collective-permute-start.8) | collective-permute-done | bytes 65568 | tf_op jit(solution)/shard_map/ppermute | solution.py:491
  102.1 2.0 %collective-permute-start.10 = (f32[8,256]{1,0:T(8,128)S(1)}, f32[8,256]{1,0:T(8,128)S(1)}, u32[]{:S(2)}, u32[]{:S(2)}) collective-permute-start(f32[8,256]{1,0:T(8,128)S(1)} %get-tuple-element.45), channel_id=1, source_target_pairs={{0,2},{1,3},{2,0},{3,1},{4,6},{5,7},{6,4},{7,5},{8,10},{9,11},{10,... | collective-permute-start | bytes 24584 | tf_op jit(solution)/shard_map/ppermute | solution.py:491
  106.1 2.5 %collective-permute-start.13 = (f32[8,256]{1,0:T(8,128)S(1)}, f32[8,256]{1,0:T(8,128)S(1)}, u32[]{:S(2)}, u32[]{:S(2)}) collective-permute-start(f32[8,256]{1,0:T(8,128)S(1)} %get-tuple-element.48), channel_id=1, source_target_pairs={{0,5},{1,4},{2,7},{3,6},{4,1},{5,0},{6,3},{7,2},{8,13},{9,12},{10,... | collective-permute-start | bytes 24584 | tf_op jit(solution)/shard_map/ppermute | solution.py:491
  108.6 2.5 %collective-permute-start.14 = (f32[8,256]{1,0:T(8,128)S(1)}, f32[8,256]{1,0:T(8,128)S(1)}, u32[]{:S(2)}, u32[]{:S(2)}) collective-permute-start(f32[8,256]{1,0:T(8,128)S(1)} %get-tuple-element.49), channel_id=1, source_target_pairs={{0,6},{1,7},{2,4},{3,5},{4,2},{5,3},{6,0},{7,1},{8,14},{9,15},{10,... | collective-permute-start | bytes 24584 | tf_op jit(solution)/shard_map/ppermute | solution.py:491
  111.1 1.4 %collective-permute-start.15 = (f32[8,256]{1,0:T(8,128)S(1)}, f32[8,256]{1,0:T(8,128)S(1)}, u32[]{:S(2)}, u32[]{:S(2)}) collective-permute-start(f32[8,256]{1,0:T(8,128)S(1)} %get-tuple-element.50), channel_id=1, source_target_pairs={{0,7},{1,6},{2,5},{3,4},{4,3},{5,2},{6,1},{7,0},{8,15},{9,14},{10,... | collective-permute-start | bytes 24584 | tf_op jit(solution)/shard_map/ppermute | solution.py:491
  113.4 3.4 %collective-permute-done.15.refs_7_ = f32[8,256]{1,0:T(8,128)S(1)} collective-permute-done((f32[8,256]{1,0:T(8,128)S(1)}, f32[8,256]{1,0:T(8,128)S(1)}, u32[]{:S(2)}, u32[]{:S(2)}) %collective-permute-start.15) | collective-permute-done | bytes 8224 | tf_op jit(solution)/shard_map/ppermute | solution.py:491
  118.0 1.4 %unpack.1 = (bf16[128,5120]{1,0:T(8,128)(2,1)}, bf16[128,1024]{1,0:T(8,128)(2,1)}, bf16[128,1024]{1,0:T(8,128)(2,1)}) custom-call(bf16[8,128,896]{2,1,0:T(8,128)(2,1)S(1)} %all-to-all-done.1.back_ref), custom_call_target="tpu_custom_call" | custom-call | tf_op jit(solution)/shard_map/unpack/pallas_call | solution.py:142
  (28 shorter events, 8.4 us)
Async XLA Ops:
  4.9 44.1 %all-to-all-start = ((bf16[8,1552,128]{2,1,0:T(8,128)(2,1)}), bf16[8,1552,128]{2,1,0:T(8,128)(2,1)S(1)}, u32[]{:S(2)}, u32[]{:S(2)}) async-start(bf16[8,1552,128]{2,1,0:T(8,128)(2,1)} %pack.1), calls=%async_computation | async-start | bytes 6356992 | tf_op jit(solution)/shard_map/all_to_all | solution.py:518
  11.2 5.3 %collective-permute-start = (bf16[1,64,256]{2,1,0:T(8,128)(2,1)S(1)}, bf16[1,64,256]{2,1,0:T(8,128)(2,1)S(1)}, u32[]{:S(2)}, u32[]{:S(2)}) collective-permute-start(bf16[1,64,256]{2,1,0:T(8,128)(2,1)S(1)} %maximum_bitcast_fusion.1), channel_id=1, source_target_pairs={{0,17},{1,16},{2,19},{3,18},{4,21},{5,20},{6,23},{7,22},{8,25},{9,... | collective-permute-start | bytes 98312 | tf_op jit(solution)/shard_map/ppermute | solution.py:501
  16.4 1.3 %collective-permute-start.1 = (bf16[2,64,256]{2,1,0:T(8,128)(2,1)S(1)}, bf16[2,64,256]{2,1,0:T(8,128)(2,1)S(1)}, u32[]{:S(2)}, u32[]{:S(2)}) collective-permute-start(bf16[2,64,256]{2,1,0:T(8,128)(2,1)S(1)} %pad_maximum_fusion.2), channel_id=1, source_target_pairs={{0,8},{8,0},{16,24},{24,16},{32,40},{40,32},{48,56},{56,48},{64,72... | collective-permute-start | bytes 196616 | tf_op jit(solution)/shard_map/ppermute | solution.py:491
  17.8 5.8 %collective-permute-start.2 = (bf16[4,64,256]{2,1,0:T(8,128)(2,1)S(1)}, bf16[4,64,256]{2,1,0:T(8,128)(2,1)S(1)}, u32[]{:S(2)}, u32[]{:S(2)}) collective-permute-start(bf16[4,64,256]{2,1,0:T(8,128)(2,1)S(1)} %pad_maximum_fusion.1), channel_id=1, source_target_pairs={{0,32},{8,40},{16,48},{24,56},{32,0},{40,8},{48,16},{56,24},{64,96... | collective-permute-start | bytes 393224 | tf_op jit(solution)/shard_map/ppermute | solution.py:491
  23.6 9.7 %collective-permute-start.3 = (bf16[8,64,256]{2,1,0:T(8,128)(2,1)S(1)}, bf16[8,64,256]{2,1,0:T(8,128)(2,1)}, u32[]{:S(2)}, u32[]{:S(2)}) collective-permute-start(bf16[8,64,256]{2,1,0:T(8,128)(2,1)S(1)} %pad_maximum_fusion.pkv_low), channel_id=1, source_target_pairs={{0,64},{8,72},{16,80},{24,88},{32,96},{40,104},{48,112},{56,120},{... | collective-permute-start | bytes 786440 | tf_op jit(solution)/shard_map/ppermute | solution.py:491
  71.0 9.7 %collective-permute-start.4 = (bf16[8,64,256]{2,1,0:T(8,128)(2,1)}, bf16[8,64,256]{2,1,0:T(8,128)(2,1)S(1)}, u32[]{:S(2)}, u32[]{:S(2)}) collective-permute-start(bf16[8,64,256]{2,1,0:T(8,128)(2,1)} %get-tuple-element.36), channel_id=1, source_target_pairs={{0,16},{8,24},{16,0},{24,8},{32,48},{40,56},{48,32},{56,40},{64,80... | collective-permute-start | bytes 786440 | tf_op jit(solution)/shard_map/ppermute | solution.py:491
  71.1 9.6 %copy-start = (bf16[8,64,256]{2,1,0:T(8,128)(2,1)S(1)}, bf16[8,64,256]{2,1,0:T(8,128)(2,1)}, u32[]{:S(2)}) copy-start(bf16[8,64,256]{2,1,0:T(8,128)(2,1)} %get-tuple-element.35.mine_ref) | copy-start | bytes 786436
  71.1 46.9 %all-to-all-start.1 = ((bf16[8,128,896]{2,1,0:T(8,128)(2,1)}), bf16[8,128,896]{2,1,0:T(8,128)(2,1)S(1)}, u32[]{:S(2)}, u32[]{:S(2)}) async-start(bf16[8,128,896]{2,1,0:T(8,128)(2,1)} %bitcast.15), calls=%async_computation.1 | async-start | bytes 3670016 | tf_op jit(solution)/shard_map/all_to_all | solution.py:528
  81.3 1.6 %collective-permute-start.5 = (f32[4,64,256]{2,1,0:T(8,128)S(1)}, f32[4,64,256]{2,1,0:T(8,128)S(1)}, u32[]{:S(2)}, u32[]{:S(2)}) collective-permute-start(f32[4,64,256]{2,1,0:T(8,128)S(1)} %get-tuple-element.38), channel_id=1, source_target_pairs={{0,8},{8,0},{16,24},{24,16},{32,40},{40,32},{48,56},{56,48},{64,72... | collective-permute-start | bytes 786440 | tf_op jit(solution)/shard_map/ppermute | solution.py:491
  83.5 12.2 %collective-permute-start.6 = (f32[64,256]{1,0:T(8,128)S(1)}, f32[64,256]{1,0:T(8,128)S(1)}, u32[]{:S(2)}, u32[]{:S(2)}) collective-permute-start(f32[64,256]{1,0:T(8,128)S(1)} %get-tuple-element.40), channel_id=1, source_target_pairs={{0,32},{8,40},{16,48},{24,56},{32,0},{40,8},{48,16},{56,24},{64,96... | collective-permute-start | bytes 196616 | tf_op jit(solution)/shard_map/ppermute | solution.py:491
  92.9 6.0 %collective-permute-start.7 = (f32[64,256]{1,0:T(8,128)S(1)}, f32[64,256]{1,0:T(8,128)S(1)}, u32[]{:S(2)}, u32[]{:S(2)}) collective-permute-start(f32[64,256]{1,0:T(8,128)S(1)} %get-tuple-element.41), channel_id=1, source_target_pairs={{0,64},{8,72},{16,80},{24,88},{32,96},{40,104},{48,112},{56,120},{... | collective-permute-start | bytes 196616 | tf_op jit(solution)/shard_map/ppermute | solution.py:491
  95.2 5.5 %collective-permute-start.8 = (f32[64,256]{1,0:T(8,128)S(1)}, f32[64,256]{1,0:T(8,128)S(1)}, u32[]{:S(2)}, u32[]{:S(2)}) collective-permute-start(f32[64,256]{1,0:T(8,128)S(1)} %get-tuple-element.42), channel_id=1, source_target_pairs={{0,96},{8,104},{16,112},{24,120},{32,64},{40,72},{48,80},{56,88},{... | collective-permute-start | bytes 196616 | tf_op jit(solution)/shard_map/ppermute | solution.py:491
  101.3 7.3 %collective-permute-start.9 = (f32[8,256]{1,0:T(8,128)S(1)}, f32[8,256]{1,0:T(8,128)S(1)}, u32[]{:S(2)}, u32[]{:S(2)}) collective-permute-start(f32[8,256]{1,0:T(8,128)S(1)} %get-tuple-element.44), channel_id=1, source_target_pairs={{0,1},{1,0},{2,3},{3,2},{4,5},{5,4},{6,7},{7,6},{8,9},{9,8},{10,11... | collective-permute-start | bytes 24584 | tf_op jit(solution)/shard_map/ppermute | solution.py:491
  102.1 9.0 %collective-permute-start.10 = (f32[8,256]{1,0:T(8,128)S(1)}, f32[8,256]{1,0:T(8,128)S(1)}, u32[]{:S(2)}, u32[]{:S(2)}) collective-permute-start(f32[8,256]{1,0:T(8,128)S(1)} %get-tuple-element.45), channel_id=1, source_target_pairs={{0,2},{1,3},{2,0},{3,1},{4,6},{5,7},{6,4},{7,5},{8,10},{9,11},{10,... | collective-permute-start | bytes 24584 | tf_op jit(solution)/shard_map/ppermute | solution.py:491
  104.1 8.4 %collective-permute-start.11 = (f32[8,256]{1,0:T(8,128)S(1)}, f32[8,256]{1,0:T(8,128)S(1)}, u32[]{:S(2)}, u32[]{:S(2)}) collective-permute-start(f32[8,256]{1,0:T(8,128)S(1)} %get-tuple-element.46), channel_id=1, source_target_pairs={{0,3},{1,2},{2,1},{3,0},{4,7},{5,6},{6,5},{7,4},{8,11},{9,10},{10,... | collective-permute-start | bytes 24584 | tf_op jit(solution)/shard_map/ppermute | solution.py:491
  104.8 7.7 %collective-permute-start.12 = (f32[8,256]{1,0:T(8,128)S(1)}, f32[8,256]{1,0:T(8,128)S(1)}, u32[]{:S(2)}, u32[]{:S(2)}) collective-permute-start(f32[8,256]{1,0:T(8,128)S(1)} %get-tuple-element.47), channel_id=1, source_target_pairs={{0,4},{1,5},{2,6},{3,7},{4,0},{5,1},{6,2},{7,3},{8,12},{9,13},{10,... | collective-permute-start | bytes 24584 | tf_op jit(solution)/shard_map/ppermute | solution.py:491
  106.1 6.4 %collective-permute-start.13 = (f32[8,256]{1,0:T(8,128)S(1)}, f32[8,256]{1,0:T(8,128)S(1)}, u32[]{:S(2)}, u32[]{:S(2)}) collective-permute-start(f32[8,256]{1,0:T(8,128)S(1)} %get-tuple-element.48), channel_id=1, source_target_pairs={{0,5},{1,4},{2,7},{3,6},{4,1},{5,0},{6,3},{7,2},{8,13},{9,12},{10,... | collective-permute-start | bytes 24584 | tf_op jit(solution)/shard_map/ppermute | solution.py:491
  108.6 4.9 %collective-permute-start.14 = (f32[8,256]{1,0:T(8,128)S(1)}, f32[8,256]{1,0:T(8,128)S(1)}, u32[]{:S(2)}, u32[]{:S(2)}) collective-permute-start(f32[8,256]{1,0:T(8,128)S(1)} %get-tuple-element.49), channel_id=1, source_target_pairs={{0,6},{1,7},{2,4},{3,5},{4,2},{5,3},{6,0},{7,1},{8,14},{9,15},{10,... | collective-permute-start | bytes 24584 | tf_op jit(solution)/shard_map/ppermute | solution.py:491
  111.1 5.8 %collective-permute-start.15 = (f32[8,256]{1,0:T(8,128)S(1)}, f32[8,256]{1,0:T(8,128)S(1)}, u32[]{:S(2)}, u32[]{:S(2)}) collective-permute-start(f32[8,256]{1,0:T(8,128)S(1)} %get-tuple-element.50), channel_id=1, source_target_pairs={{0,7},{1,6},{2,5},{3,4},{4,3},{5,2},{6,1},{7,0},{8,15},{9,14},{10,... | collective-permute-start | bytes 24584 | tf_op jit(solution)/shard_map/ppermute | solution.py:491
where the time goes:
time: 120 us
  waiting for transfers between devices  44.4 us (37%)
  starting transfers between devices  42 us (35%)
  Pallas kernels  30.7 us (26%)
  between operations  1.57 us (1%)
    ppermute x15, starting transfers between devices, swap(): lax.ppermute(value, axis, [(i, i ^ d) for i in range(lax.axis_size(axis))])  29.5 us
    ppermute x15, waiting for transfers between devices, swap(): lax.ppermute(value, axis, [(i, i ^ d) for i in range(lax.axis_size(axis))])  26.9 us
    pallas_call x1, Pallas kernels, attend(): pl.pallas_call(attend_kernel, in_specs=[SMEM, VMEM, ANY, ANY], out_specs=...  22 us
    all_to_all x1, waiting for transfers between devices, local(): x = lax.all_to_all(send, 'resp', 0, 0, tiled=True)  15.6 us
    all_to_all x1, starting transfers between devices, local(): x = lax.all_to_all(send, 'resp', 0, 0, tiled=True)  5.49 us
    pallas_call x1, Pallas kernels, pack(): pl.pallas_call(pack_kernel, in_specs=[HBM] * 5, out_specs=HBM, out_shape=...  4.25 us
    all_to_all x1, starting transfers between devices, local(): lax.all_to_all(back.reshape(KV_HEADS, rows, BACK_W), 'resp', 0, 0, tiled=...  3.74 us
    ppermute x1, starting transfers between devices, swap_across(): return lax.ppermute(value, ('prefix', 'resp'), pairs)  3.37 us
  transfers between devices with their start and end apart: 18, of which 11 were waited for; matrix products, arithmetic and copies ran while one was open for 1% of the time, Pallas kernels for 3%

commit v1 on v0

--- a/solution.py
+++ b/solution.py
@@ -154,7 +154,8 @@
     )(back)
 
 
-def attend_kernel(place_ref, x_ref, pkv_low, pkv_high, back_out, pg_keep, pg_give, *refs):
+def attend_kernel(place_ref, x_ref, pkv_low, pkv_high, back_out, *refs):
+    pg_outs, refs = refs[:4], refs[4:]
     pkv_ref, back_ref, pg_ref, sems, block_sems, k_all, v_all, k_t = refs[:8]
     p_s, l_s, dq_t, dk, dv = refs[8:13]
     sets = [refs[13:20], refs[20:27]]
@@ -334,14 +335,17 @@
         def _():
             leaving(i).start()
 
-    pg_ref[:, 0:HEAD_DIM] = (dk[0:prompt] * SCALE).astype(BF16)
-    pg_ref[:, HEAD_DIM:] = dv[0:prompt].astype(BF16)
+    for n, (total, scale) in enumerate(((dk, SCALE), (dv, 1.0))):
+        runs = (total[0:prompt] * scale).reshape(-1, 2, 8, HEAD_DIM)
+        for lo in range(2):
+            pg_ref[lo, :, n * HEAD_DIM : (n + 1) * HEAD_DIM] = runs[:, lo].reshape(prompt // 2, HEAD_DIM).astype(BF16)
     back_ref[:, QW : QW + HEAD_DIM] = (dk[prompt:] * SCALE).astype(BF16)
     back_ref[:, QW + HEAD_DIM :] = dv[prompt:].astype(BF16)
-    mine = me_prefix & X_BIT
+    mine, low = me_prefix & X_BIT, place_ref[2] & 1
+    kept = share // 2
     copies = [
-        (pg_ref.at[pl.ds(times(f + (f & -X_BIT) + (mine ^ bit), share), share)], out.at[f])
-        for bit, out in ((0, pg_keep), (X_BIT, pg_give))
+        (pg_ref.at[low ^ flip_low, pl.ds(times(f + (f & -X_BIT) + (mine ^ bit), kept), kept)], out.at[f])
+        for (bit, flip_low), out in zip(((0, 0), (X_BIT, 0), (0, 1), (X_BIT, 1)), pg_outs)
         for f in range(half)
     ]
     copies = start_all([(back_ref.at[:, QW:], back_out.at[:, QW:])] + copies, sems)
@@ -358,7 +362,7 @@
     prompt = responses * share
     keys = slots + prompt
     wide = GROUP * TILE
-    outs = [((slots, BACK_W), BF16)] + [((half, share, prompt_width), BF16)] * 2
+    outs = [((slots, BACK_W), BF16)] + [((half, share // 2, prompt_width), BF16)] * 4
     stats = pltpu.VMEM((keys // TILE * STATS, wide), F32)
     one_set = [
         pltpu.VMEM((wide, HEAD_DIM), BF16),
@@ -377,8 +381,8 @@
         scratch_shapes=[
             pltpu.VMEM((prompt, prompt_width), BF16),
             pltpu.VMEM((slots, BACK_W), BF16),
-            pltpu.VMEM((prompt, prompt_width), BF16),
-            pltpu.SemaphoreType.DMA((1 + responses,)),
+            pltpu.VMEM((2, prompt // 2, prompt_width), BF16),
+            pltpu.SemaphoreType.DMA((1 + 2 * responses,)),
             pltpu.SemaphoreType.DMA((slots // TILE,)),
             pltpu.VMEM((keys, HEAD_DIM), BF16),
             pltpu.VMEM((keys, 2 * HEAD_DIM), BF16),
@@ -398,27 +402,29 @@
     )(place, pltpu.with_memory_space_constraint(x, pltpu.VMEM), *pkv)
 
 
-def core_kernel(place_ref, mine_ref, got_ref, keep_ref, give_ref, total):
-    total[...] = mine_ref[...].astype(F32) + got_ref[...].astype(F32)
-    core = place_ref[1] & CORE_BIT
+def core_kernel(place_ref, mine_ref, over_x_ref, low_ref, both_ref, keep_ref, give_ref, total):
+    width = mine_ref.shape[2]
+    core, low = place_ref[1] & CORE_BIT, place_ref[2] & 1
+    total[:, :, pl.ds(times(low, width), width)] = mine_ref[...].astype(F32) + over_x_ref[...].astype(F32)
+    total[:, :, pl.ds(times(1 - low, width), width)] = low_ref[...].astype(F32) + both_ref[...].astype(F32)
     for f in range(keep_ref.shape[0]):
         keep_ref[f] = total[2 * f + core]
         give_ref[f] = total[2 * f + 1 - core]
 
 
-def sum_over_x(place, mine, got):
-    count, share, width = mine.shape
-    part = jax.ShapeDtypeStruct((count // 2, share, width), F32)
+def sum_over_x(place, parts):
+    count, share, width = parts[0].shape
+    part = jax.ShapeDtypeStruct((count // 2, share, 2 * width), F32)
     return pl.pallas_call(
         core_kernel,
-        in_specs=[SMEM, VMEM, VMEM],
+        in_specs=[SMEM] + [VMEM] * 4,
         out_specs=[VMEM] * 2,
         out_shape=[part] * 2,
-        scratch_shapes=[pltpu.VMEM(mine.shape, F32)],
+        scratch_shapes=[pltpu.VMEM((count, share, 2 * width), F32)],
         compiler_params=params(8),
         cost_estimate=pl.CostEstimate(flops=5 * 10**10, transcendentals=0, bytes_accessed=2**20),
         name="sum_over_x",
-    )(place, mine, got)
+    )(place, *parts)
 
 
 def z_kernel(place_ref, mine_ref, got_ref, *refs):
@@ -443,43 +449,45 @@
 
 
 def sum_kernel(place_ref, *refs):
-    parts, outs, total = refs[: -KV_HEADS - 1], refs[-KV_HEADS - 1 : -1], refs[-1]
+    parts, outs, total = refs[:4], refs[4:-1], refs[-1]
     value = parts[0][...]
     for part in parts[1:]:
         value = value + part[...]
     total[...] = value
     own = outs[0].shape[0]
     for d, out in enumerate(outs):
-        out[...] = total[pl.ds(times(place_ref[2] ^ d, own), own)]
-
-
-def sum_parts(place, parts):
+        out[...] = total[pl.ds(times((place_ref[2] // 2) ^ d, own), own)]
+
+
+def sum_over_z(place, parts):
     rows, width = parts[0].shape
-    own = rows // KV_HEADS
+    count = KV_HEADS // 2
     return pl.pallas_call(
         sum_kernel,
         in_specs=[SMEM] + [VMEM] * len(parts),
-        out_specs=[VMEM] * KV_HEADS,
-        out_shape=[jax.ShapeDtypeStruct((own, width), F32)] * KV_HEADS,
+        out_specs=[VMEM] * count,
+        out_shape=[jax.ShapeDtypeStruct((rows // count, width), F32)] * count,
         scratch_shapes=[pltpu.VMEM((rows, width), F32)],
         compiler_params=params(4),
-        name="sum_parts",
+        name="sum_over_z",
     )(place, *parts)
 
 
 def spread_kernel(place_ref, *refs):
-    parts, (k_ref, v_ref) = refs[:KV_HEADS], refs[KV_HEADS:]
+    parts, (k_ref, v_ref) = refs[:-2], refs[-2:]
     for d, part in enumerate(parts):
-        cols = pl.ds(times(place_ref[2] ^ d, HEAD_DIM), HEAD_DIM)
-        k_ref[:, cols] = part[:, 0:HEAD_DIM].astype(BF16)
-        v_ref[:, cols] = part[:, HEAD_DIM:].astype(BF16)
+        for low in range(2):
+            cols = pl.ds(times(((place_ref[2] // 2) ^ d) * 2 + low, HEAD_DIM), HEAD_DIM)
+            at = 2 * low * HEAD_DIM
+            k_ref[:, cols] = part[:, at : at + HEAD_DIM].astype(BF16)
+            v_ref[:, cols] = part[:, at + HEAD_DIM : at + 2 * HEAD_DIM].astype(BF16)
 
 
 def spread_heads(place, parts):
     shape = jax.ShapeDtypeStruct((parts[0].shape[0], KV_HEADS * HEAD_DIM), BF16)
     return pl.pallas_call(
         spread_kernel,
-        in_specs=[SMEM] + [VMEM] * KV_HEADS,
+        in_specs=[SMEM] + [VMEM] * len(parts),
         out_specs=[VMEM] * 2,
         out_shape=[shape] * 2,
         compiler_params=params(4),
@@ -524,12 +532,13 @@
     for bit in GATHER_BITS[1:-1]:
         pkv = jnp.concatenate([pkv, swap(pkv, "prefix", 1 << bit)])
     pkv = [pkv, swap(pkv, "prefix", 1 << GATHER_BITS[-1])]
-    back, keep, give = attend(place, x, pkv)
+    back, *parts = attend(place, x, pkv)
     back = lax.all_to_all(back.reshape(KV_HEADS, rows, BACK_W), "resp", 0, 0, tiled=True)
-    keep, give = sum_over_x(place, keep, swap(give, "prefix", X_BIT))
+    parts = [parts[0], swap(parts[1], "prefix", X_BIT), swap(parts[2], "resp", 1), swap_across(parts[3])]
+    keep, give = sum_over_x(place, parts)
     parts = sum_over_cores(place, keep, swap(give, "prefix", CORE_BIT))
-    parts = swap_all(sum_parts(place, swap_all(parts, "prefix", 2 * X_BIT)), "resp")
-    total = spread_heads(place, parts)
+    parts = sum_over_z(place, swap_all(parts, "prefix", 2 * X_BIT))
+    total = spread_heads(place, swap_all(parts, "resp", 2))
     grad_query, grad_keys, grad_values = unpack(back)
     return (grad_query[None], grad_keys[None], grad_values[None], total[0], total[1])
 

time: 120 us -> 112 us (0.933)
  starting transfers between devices: 42 us -> 32.3 us
  Pallas kernels: 30.7 us -> 38.1 us
  waiting for transfers between devices: 44.4 us -> 39.3 us
    ppermute x15 -> x12, starting transfers between devices: 29.5 us -> 16.5 us  [swap(): lax.ppermute(value, axis, [(i, i ^ d) for i in range(lax.axis_size(axis))])]
    pallas_call x1, Pallas kernels: 22 us -> 29.5 us  [attend(): pl.pallas_call(attend_kernel, in_specs=[SMEM, VMEM, ANY, ANY], out_specs=...]
    ppermute x15 -> x12, waiting for transfers between devices: 26.9 us -> 20.4 us  [swap(): lax.ppermute(value, axis, [(i, i ^ d) for i in range(lax.axis_size(axis))])]
    ppermute x1 -> x2, starting transfers between devices: 3.37 us -> 6.56 us  [swap_across(): return lax.ppermute(value, ('prefix', 'resp'), pairs)]
    ppermute x1 -> x2, waiting for transfers between devices: 1.89 us -> 3.23 us  [swap_across(): return lax.ppermute(value, ('prefix', 'resp'), pairs)]
  transfers between devices with their start and end apart: 18 -> 16, of which waited for: 11 -> 12; matrix products, arithmetic and copies ran while one was open for 1% -> 1% of each run, Pallas kernels for 3% -> 3%
where the time goes in v1:
time: 112 us
  waiting for transfers between devices  39.3 us (35%)
  Pallas kernels  38.1 us (34%)
  starting transfers between devices  32.3 us (29%)
  between operations  1.57 us (1%)
    pallas_call x1, Pallas kernels, attend(): pl.pallas_call(attend_kernel, in_specs=[SMEM, VMEM, ANY, ANY], out_specs=...  29.5 us
    ppermute x12, waiting for transfers between devices, swap(): lax.ppermute(value, axis, [(i, i ^ d) for i in range(lax.axis_size(axis))])  20.4 us
    ppermute x12, starting transfers between devices, swap(): lax.ppermute(value, axis, [(i, i ^ d) for i in range(lax.axis_size(axis))])  16.5 us
    all_to_all x1, waiting for transfers between devices, local(): x = lax.all_to_all(send, 'resp', 0, 0, tiled=True)  15.6 us
    ppermute x2, starting transfers between devices, swap_across(): return lax.ppermute(value, ('prefix', 'resp'), pairs)  6.56 us
    all_to_all x1, starting transfers between devices, local(): x = lax.all_to_all(send, 'resp', 0, 0, tiled=True)  5.49 us
    pallas_call x1, Pallas kernels, pack(): pl.pallas_call(pack_kernel, in_specs=[HBM] * 5, out_specs=HBM, out_shape=...  4.25 us
    all_to_all x1, starting transfers between devices, local(): lax.all_to_all(back.reshape(KV_HEADS, rows, BACK_W), 'resp', 0, 0, tiled=...  3.72 us
  transfers between devices with their start and end apart: 16, of which 12 were waited for; matrix products, arithmetic and copies ran while one was open for 1% of the time, Pallas kernels for 3%

profile of v1, /device:TPU:0, one launch (start us, length us, event | category | flops | bytes accessed | tf_op | source)
XLA Modules:
  0.0 112.2 jit_solution(10758476973026596103)
XLA Ops:
  0.6 4.3 %pack.1 = bf16[8,1552,128]{2,1,0:T(8,128)(2,1)} custom-call(bf16[128,5120]{1,0:T(8,128)(2,1)} %bitcast.16, bf16[128,5120]{1,0:T(8,128)(2,1)} %bitcast.17, bf16[128,5120]{1,0:T(8,128)(2,1)} %bitcast.18, bf16[128,1024]{1,0:T(8,128)(2,1)} %bitcast.19, bf16[128,1024]{1,0:T(8,128)(2,1)} %bitcast.20), custom_call_target="tpu_custom_call" | custom-call | tf_op jit(solution)/shard_map/pack/pallas_call | solution.py:111
  4.9 5.5 %all-to-all-start = ((bf16[8,1552,128]{2,1,0:T(8,128)(2,1)}), bf16[8,1552,128]{2,1,0:T(8,128)(2,1)S(1)}, u32[]{:S(2)}, u32[]{:S(2)}) async-start(bf16[8,1552,128]{2,1,0:T(8,128)(2,1)} %pack.1), calls=%async_computation | async-start | bytes 6356992 | tf_op jit(solution)/shard_map/all_to_all | solution.py:526
  11.2 3.4 %collective-permute-start = (bf16[1,64,256]{2,1,0:T(8,128)(2,1)S(1)}, bf16[1,64,256]{2,1,0:T(8,128)(2,1)S(1)}, u32[]{:S(2)}, u32[]{:S(2)}) collective-permute-start(bf16[1,64,256]{2,1,0:T(8,128)(2,1)S(1)} %maximum_bitcast_fusion.1), channel_id=1, source_target_pairs={{0,17},{1,16},{2,19},{3,18},{4,21},{5,20},{6,23},{7,22},{8,25},{9,... | collective-permute-start | bytes 98312 | tf_op jit(solution)/shard_map/ppermute | solution.py:509
  14.5 1.9 %collective-permute-done = bf16[1,64,256]{2,1,0:T(8,128)(2,1)S(1)} collective-permute-done((bf16[1,64,256]{2,1,0:T(8,128)(2,1)S(1)}, bf16[1,64,256]{2,1,0:T(8,128)(2,1)S(1)}, u32[]{:S(2)}, u32[]{:S(2)}) %collective-permute-start) | collective-permute-done | bytes 32800 | tf_op jit(solution)/shard_map/ppermute | solution.py:509
  16.5 1.2 %collective-permute-done.1 = bf16[2,64,256]{2,1,0:T(8,128)(2,1)S(1)} collective-permute-done((bf16[2,64,256]{2,1,0:T(8,128)(2,1)S(1)}, bf16[2,64,256]{2,1,0:T(8,128)(2,1)S(1)}, u32[]{:S(2)}, u32[]{:S(2)}) %collective-permute-start.1) | collective-permute-done | bytes 65568 | tf_op jit(solution)/shard_map/ppermute | solution.py:499
  17.8 2.0 %collective-permute-start.2 = (bf16[4,64,256]{2,1,0:T(8,128)(2,1)S(1)}, bf16[4,64,256]{2,1,0:T(8,128)(2,1)S(1)}, u32[]{:S(2)}, u32[]{:S(2)}) collective-permute-start(bf16[4,64,256]{2,1,0:T(8,128)(2,1)S(1)} %pad_maximum_fusion.1), channel_id=1, source_target_pairs={{0,32},{8,40},{16,48},{24,56},{32,0},{40,8},{48,16},{56,24},{64,96... | collective-permute-start | bytes 393224 | tf_op jit(solution)/shard_map/ppermute | solution.py:499
  19.8 3.8 %collective-permute-done.2 = bf16[4,64,256]{2,1,0:T(8,128)(2,1)S(1)} collective-permute-done((bf16[4,64,256]{2,1,0:T(8,128)(2,1)S(1)}, bf16[4,64,256]{2,1,0:T(8,128)(2,1)S(1)}, u32[]{:S(2)}, u32[]{:S(2)}) %collective-permute-start.2) | collective-permute-done | bytes 131104 | tf_op jit(solution)/shard_map/ppermute | solution.py:499
  23.6 3.8 %collective-permute-start.3 = (bf16[8,64,256]{2,1,0:T(8,128)(2,1)S(1)}, bf16[8,64,256]{2,1,0:T(8,128)(2,1)}, u32[]{:S(2)}, u32[]{:S(2)}) collective-permute-start(bf16[8,64,256]{2,1,0:T(8,128)(2,1)S(1)} %pad_maximum_fusion.pkv_low), channel_id=1, source_target_pairs={{0,64},{8,72},{16,80},{24,88},{32,96},{40,104},{48,112},{56,120},{... | collective-permute-start | bytes 786440 | tf_op jit(solution)/shard_map/ppermute | solution.py:499
  28.2 5.2 %collective-permute-done.3.pkv_high = bf16[8,64,256]{2,1,0:T(8,128)(2,1)} collective-permute-done((bf16[8,64,256]{2,1,0:T(8,128)(2,1)S(1)}, bf16[8,64,256]{2,1,0:T(8,128)(2,1)}, u32[]{:S(2)}, u32[]{:S(2)}) %collective-permute-start.3) | collective-permute-done | bytes 262176 | tf_op jit(solution)/shard_map/ppermute | solution.py:499
  33.3 15.6 %all-to-all-done.x_ref = bf16[8,1552,128]{2,1,0:T(8,128)(2,1)S(1)} async-done(((bf16[8,1552,128]{2,1,0:T(8,128)(2,1)}), bf16[8,1552,128]{2,1,0:T(8,128)(2,1)S(1)}, u32[]{:S(2)}, u32[]{:S(2)}) %all-to-all-start) | async-done | bytes 3178528 | tf_op jit(solution)/shard_map/all_to_all | solution.py:526
  48.9 29.5 %attend.1 = (bf16[1024,896]{1,0:T(8,128)(2,1)}, bf16[8,32,256]{2,1,0:T(8,128)(2,1)}, bf16[8,32,256]{2,1,0:T(8,128)(2,1)}, bf16[8,32,256]{2,1,0:T(8,128)(2,1)}, bf16[8,32,256]{2,1,0:T(8,128)(2,1)}) custom-call(s32[3]{0:T(128)S(1)} %pad_add_fusion.place_ref, bf16[8,1552,128]{2,1,0:T(8,128)(2,1)S(1)} %all-to-all-done.x_ref, ...), custom_call_target="tpu_custom_call" | custom-call | flops 13421772800 | bytes 5242880 | tf_op jit(solution)/shard_map/attend/pallas_call | solution.py:376
  79.4 3.2 %collective-permute-start.6 = (bf16[8,32,256]{2,1,0:T(8,128)(2,1)}, bf16[8,32,256]{2,1,0:T(8,128)(2,1)S(1)}, u32[]{:S(2)}, u32[]{:S(2)}) collective-permute-start(bf16[8,32,256]{2,1,0:T(8,128)(2,1)} %get-tuple-element.36), channel_id=1, source_target_pairs={{0,17},{1,16},{2,19},{3,18},{4,21},{5,20},{6,23},{7,22},{8,25},{9,... | collective-permute-start | bytes 393224 | tf_op jit(solution)/shard_map/ppermute | solution.py:509
  82.6 3.7 %all-to-all-start.1 = ((bf16[8,128,896]{2,1,0:T(8,128)(2,1)}), bf16[8,128,896]{2,1,0:T(8,128)(2,1)S(1)}, u32[]{:S(2)}, u32[]{:S(2)}) async-start(bf16[8,128,896]{2,1,0:T(8,128)(2,1)} %bitcast.15), calls=%async_computation.1 | async-start | bytes 3670016 | tf_op jit(solution)/shard_map/all_to_all | solution.py:536
  86.5 1.3 %collective-permute-done.6.both_ref = bf16[8,32,256]{2,1,0:T(8,128)(2,1)S(1)} collective-permute-done((bf16[8,32,256]{2,1,0:T(8,128)(2,1)}, bf16[8,32,256]{2,1,0:T(8,128)(2,1)S(1)}, u32[]{:S(2)}, u32[]{:S(2)}) %collective-permute-start.6) | collective-permute-done | bytes 131104 | tf_op jit(solution)/shard_map/ppermute | solution.py:509
  88.6 1.5 %collective-permute-done.7.got_ref = f32[4,32,512]{2,1,0:T(8,128)S(1)} collective-permute-done((f32[4,32,512]{2,1,0:T(8,128)S(1)}, f32[4,32,512]{2,1,0:T(8,128)S(1)}, u32[]{:S(2)}, u32[]{:S(2)}) %collective-permute-start.7) | collective-permute-done | bytes 262176 | tf_op jit(solution)/shard_map/ppermute | solution.py:499
  90.7 2.0 %collective-permute-start.8 = (f32[32,512]{1,0:T(8,128)S(1)}, f32[32,512]{1,0:T(8,128)S(1)}, u32[]{:S(2)}, u32[]{:S(2)}) collective-permute-start(f32[32,512]{1,0:T(8,128)S(1)} %get-tuple-element.40), channel_id=1, source_target_pairs={{0,32},{8,40},{16,48},{24,56},{32,0},{40,8},{48,16},{56,24},{64,96... | collective-permute-start | bytes 196616 | tf_op jit(solution)/shard_map/ppermute | solution.py:499
  93.0 2.5 %collective-permute-start.10 = (f32[32,512]{1,0:T(8,128)S(1)}, f32[32,512]{1,0:T(8,128)S(1)}, u32[]{:S(2)}, u32[]{:S(2)}) collective-permute-start(f32[32,512]{1,0:T(8,128)S(1)} %get-tuple-element.42), channel_id=1, source_target_pairs={{0,96},{8,104},{16,112},{24,120},{32,64},{40,72},{48,80},{56,88},{... | collective-permute-start | bytes 196616 | tf_op jit(solution)/shard_map/ppermute | solution.py:499
  95.5 3.0 %collective-permute-done.9.refs_2_ = f32[32,512]{1,0:T(8,128)S(1)} collective-permute-done((f32[32,512]{1,0:T(8,128)S(1)}, f32[32,512]{1,0:T(8,128)S(1)}, u32[]{:S(2)}, u32[]{:S(2)}) %collective-permute-start.9) | collective-permute-done | bytes 65568 | tf_op jit(solution)/shard_map/ppermute | solution.py:499
  100.1 1.3 %collective-permute-start.11 = (f32[8,512]{1,0:T(8,128)S(1)}, f32[8,512]{1,0:T(8,128)S(1)}, u32[]{:S(2)}, u32[]{:S(2)}) collective-permute-start(f32[8,512]{1,0:T(8,128)S(1)} %get-tuple-element.44), channel_id=1, source_target_pairs={{0,2},{1,3},{2,0},{3,1},{4,6},{5,7},{6,4},{7,5},{8,10},{9,11},{10,... | collective-permute-start | bytes 49160 | tf_op jit(solution)/shard_map/ppermute | solution.py:499
  101.3 2.3 %collective-permute-start.12 = (f32[8,512]{1,0:T(8,128)S(1)}, f32[8,512]{1,0:T(8,128)S(1)}, u32[]{:S(2)}, u32[]{:S(2)}) collective-permute-start(f32[8,512]{1,0:T(8,128)S(1)} %get-tuple-element.45), channel_id=1, source_target_pairs={{0,4},{1,5},{2,6},{3,7},{4,0},{5,1},{6,2},{7,3},{8,12},{9,13},{10,... | collective-permute-start | bytes 49160 | tf_op jit(solution)/shard_map/ppermute | solution.py:499
  103.6 1.2 %collective-permute-start.13 = (f32[8,512]{1,0:T(8,128)S(1)}, f32[8,512]{1,0:T(8,128)S(1)}, u32[]{:S(2)}, u32[]{:S(2)}) collective-permute-start(f32[8,512]{1,0:T(8,128)S(1)} %get-tuple-element.46), channel_id=1, source_target_pairs={{0,6},{1,7},{2,4},{3,5},{4,2},{5,3},{6,0},{7,1},{8,14},{9,15},{10,... | collective-permute-start | bytes 49160 | tf_op jit(solution)/shard_map/ppermute | solution.py:499
  104.8 2.5 %collective-permute-done.11.refs_1_ = f32[8,512]{1,0:T(8,128)S(1)} collective-permute-done((f32[8,512]{1,0:T(8,128)S(1)}, f32[8,512]{1,0:T(8,128)S(1)}, u32[]{:S(2)}, u32[]{:S(2)}) %collective-permute-start.11) | collective-permute-done | bytes 16416 | tf_op jit(solution)/shard_map/ppermute | solution.py:499
  107.4 2.0 %collective-permute-done.13.refs_3_ = f32[8,512]{1,0:T(8,128)S(1)} collective-permute-done((f32[8,512]{1,0:T(8,128)S(1)}, f32[8,512]{1,0:T(8,128)S(1)}, u32[]{:S(2)}, u32[]{:S(2)}) %collective-permute-start.13) | collective-permute-done | bytes 16416 | tf_op jit(solution)/shard_map/ppermute | solution.py:499
  110.6 1.4 %unpack.1 = (bf16[128,5120]{1,0:T(8,128)(2,1)}, bf16[128,1024]{1,0:T(8,128)(2,1)}, bf16[128,1024]{1,0:T(8,128)(2,1)}) custom-call(bf16[8,128,896]{2,1,0:T(8,128)(2,1)S(1)} %all-to-all-done.1.back_ref), custom_call_target="tpu_custom_call" | custom-call | tf_op jit(solution)/shard_map/unpack/pallas_call | solution.py:142
  (24 shorter events, 6.4 us)
Async XLA Ops:
  4.9 44.1 %all-to-all-start = ((bf16[8,1552,128]{2,1,0:T(8,128)(2,1)}), bf16[8,1552,128]{2,1,0:T(8,128)(2,1)S(1)}, u32[]{:S(2)}, u32[]{:S(2)}) async-start(bf16[8,1552,128]{2,1,0:T(8,128)(2,1)} %pack.1), calls=%async_computation | async-start | bytes 6356992 | tf_op jit(solution)/shard_map/all_to_all | solution.py:526
  11.2 5.3 %collective-permute-start = (bf16[1,64,256]{2,1,0:T(8,128)(2,1)S(1)}, bf16[1,64,256]{2,1,0:T(8,128)(2,1)S(1)}, u32[]{:S(2)}, u32[]{:S(2)}) collective-permute-start(bf16[1,64,256]{2,1,0:T(8,128)(2,1)S(1)} %maximum_bitcast_fusion.1), channel_id=1, source_target_pairs={{0,17},{1,16},{2,19},{3,18},{4,21},{5,20},{6,23},{7,22},{8,25},{9,... | collective-permute-start | bytes 98312 | tf_op jit(solution)/shard_map/ppermute | solution.py:509
  16.4 1.3 %collective-permute-start.1 = (bf16[2,64,256]{2,1,0:T(8,128)(2,1)S(1)}, bf16[2,64,256]{2,1,0:T(8,128)(2,1)S(1)}, u32[]{:S(2)}, u32[]{:S(2)}) collective-permute-start(bf16[2,64,256]{2,1,0:T(8,128)(2,1)S(1)} %pad_maximum_fusion.2), channel_id=1, source_target_pairs={{0,8},{8,0},{16,24},{24,16},{32,40},{40,32},{48,56},{56,48},{64,72... | collective-permute-start | bytes 196616 | tf_op jit(solution)/shard_map/ppermute | solution.py:499
  17.8 5.8 %collective-permute-start.2 = (bf16[4,64,256]{2,1,0:T(8,128)(2,1)S(1)}, bf16[4,64,256]{2,1,0:T(8,128)(2,1)S(1)}, u32[]{:S(2)}, u32[]{:S(2)}) collective-permute-start(bf16[4,64,256]{2,1,0:T(8,128)(2,1)S(1)} %pad_maximum_fusion.1), channel_id=1, source_target_pairs={{0,32},{8,40},{16,48},{24,56},{32,0},{40,8},{48,16},{56,24},{64,96... | collective-permute-start | bytes 393224 | tf_op jit(solution)/shard_map/ppermute | solution.py:499
  23.6 9.7 %collective-permute-start.3 = (bf16[8,64,256]{2,1,0:T(8,128)(2,1)S(1)}, bf16[8,64,256]{2,1,0:T(8,128)(2,1)}, u32[]{:S(2)}, u32[]{:S(2)}) collective-permute-start(bf16[8,64,256]{2,1,0:T(8,128)(2,1)S(1)} %pad_maximum_fusion.pkv_low), channel_id=1, source_target_pairs={{0,64},{8,72},{16,80},{24,88},{32,96},{40,104},{48,112},{56,120},{... | collective-permute-start | bytes 786440 | tf_op jit(solution)/shard_map/ppermute | solution.py:499
  78.5 7.9 %collective-permute-start.4 = (bf16[8,32,256]{2,1,0:T(8,128)(2,1)}, bf16[8,32,256]{2,1,0:T(8,128)(2,1)S(1)}, u32[]{:S(2)}, u32[]{:S(2)}) collective-permute-start(bf16[8,32,256]{2,1,0:T(8,128)(2,1)} %get-tuple-element.34), channel_id=1, source_target_pairs={{0,16},{8,24},{16,0},{24,8},{32,48},{40,56},{48,32},{56,40},{64,80... | collective-permute-start | bytes 393224 | tf_op jit(solution)/shard_map/ppermute | solution.py:499
  78.6 8.0 %collective-permute-start.5 = (bf16[8,32,256]{2,1,0:T(8,128)(2,1)}, bf16[8,32,256]{2,1,0:T(8,128)(2,1)S(1)}, u32[]{:S(2)}, u32[]{:S(2)}) collective-permute-start(bf16[8,32,256]{2,1,0:T(8,128)(2,1)} %get-tuple-element.35), channel_id=1, source_target_pairs={{0,1},{1,0},{2,3},{3,2},{4,5},{5,4},{6,7},{7,6},{8,9},{9,8},{10,11... | collective-permute-start | bytes 393224 | tf_op jit(solution)/shard_map/ppermute | solution.py:499
  79.4 8.4 %collective-permute-start.6 = (bf16[8,32,256]{2,1,0:T(8,128)(2,1)}, bf16[8,32,256]{2,1,0:T(8,128)(2,1)S(1)}, u32[]{:S(2)}, u32[]{:S(2)}) collective-permute-start(bf16[8,32,256]{2,1,0:T(8,128)(2,1)} %get-tuple-element.36), channel_id=1, source_target_pairs={{0,17},{1,16},{2,19},{3,18},{4,21},{5,20},{6,23},{7,22},{8,25},{9,... | collective-permute-start | bytes 393224 | tf_op jit(solution)/shard_map/ppermute | solution.py:509
  82.6 5.2 %copy-start = (bf16[8,32,256]{2,1,0:T(8,128)(2,1)S(1)}, bf16[8,32,256]{2,1,0:T(8,128)(2,1)}, u32[]{:S(2)}) copy-start(bf16[8,32,256]{2,1,0:T(8,128)(2,1)} %get-tuple-element.33.mine_ref) | copy-start | bytes 393220
  82.6 27.9 %all-to-all-start.1 = ((bf16[8,128,896]{2,1,0:T(8,128)(2,1)}), bf16[8,128,896]{2,1,0:T(8,128)(2,1)S(1)}, u32[]{:S(2)}, u32[]{:S(2)}) async-start(bf16[8,128,896]{2,1,0:T(8,128)(2,1)} %bitcast.15), calls=%async_computation.1 | async-start | bytes 3670016 | tf_op jit(solution)/shard_map/all_to_all | solution.py:536
  88.5 1.6 %collective-permute-start.7 = (f32[4,32,512]{2,1,0:T(8,128)S(1)}, f32[4,32,512]{2,1,0:T(8,128)S(1)}, u32[]{:S(2)}, u32[]{:S(2)}) collective-permute-start(f32[4,32,512]{2,1,0:T(8,128)S(1)} %get-tuple-element.38), channel_id=1, source_target_pairs={{0,8},{8,0},{16,24},{24,16},{32,40},{40,32},{48,56},{56,48},{64,72... | collective-permute-start | bytes 786440 | tf_op jit(solution)/shard_map/ppermute | solution.py:499
  90.7 4.8 %collective-permute-start.8 = (f32[32,512]{1,0:T(8,128)S(1)}, f32[32,512]{1,0:T(8,128)S(1)}, u32[]{:S(2)}, u32[]{:S(2)}) collective-permute-start(f32[32,512]{1,0:T(8,128)S(1)} %get-tuple-element.40), channel_id=1, source_target_pairs={{0,32},{8,40},{16,48},{24,56},{32,0},{40,8},{48,16},{56,24},{64,96... | collective-permute-start | bytes 196616 | tf_op jit(solution)/shard_map/ppermute | solution.py:499
  92.7 5.8 %collective-permute-start.9 = (f32[32,512]{1,0:T(8,128)S(1)}, f32[32,512]{1,0:T(8,128)S(1)}, u32[]{:S(2)}, u32[]{:S(2)}) collective-permute-start(f32[32,512]{1,0:T(8,128)S(1)} %get-tuple-element.41), channel_id=1, source_target_pairs={{0,64},{8,72},{16,80},{24,88},{32,96},{40,104},{48,112},{56,120},{... | collective-permute-start | bytes 196616 | tf_op jit(solution)/shard_map/ppermute | solution.py:499
  93.0 6.5 %collective-permute-start.10 = (f32[32,512]{1,0:T(8,128)S(1)}, f32[32,512]{1,0:T(8,128)S(1)}, u32[]{:S(2)}, u32[]{:S(2)}) collective-permute-start(f32[32,512]{1,0:T(8,128)S(1)} %get-tuple-element.42), channel_id=1, source_target_pairs={{0,96},{8,104},{16,112},{24,120},{32,64},{40,72},{48,80},{56,88},{... | collective-permute-start | bytes 196616 | tf_op jit(solution)/shard_map/ppermute | solution.py:499
  100.1 7.3 %collective-permute-start.11 = (f32[8,512]{1,0:T(8,128)S(1)}, f32[8,512]{1,0:T(8,128)S(1)}, u32[]{:S(2)}, u32[]{:S(2)}) collective-permute-start(f32[8,512]{1,0:T(8,128)S(1)} %get-tuple-element.44), channel_id=1, source_target_pairs={{0,2},{1,3},{2,0},{3,1},{4,6},{5,7},{6,4},{7,5},{8,10},{9,11},{10,... | collective-permute-start | bytes 49160 | tf_op jit(solution)/shard_map/ppermute | solution.py:499
  101.3 6.0 %collective-permute-start.12 = (f32[8,512]{1,0:T(8,128)S(1)}, f32[8,512]{1,0:T(8,128)S(1)}, u32[]{:S(2)}, u32[]{:S(2)}) collective-permute-start(f32[8,512]{1,0:T(8,128)S(1)} %get-tuple-element.45), channel_id=1, source_target_pairs={{0,4},{1,5},{2,6},{3,7},{4,0},{5,1},{6,2},{7,3},{8,12},{9,13},{10,... | collective-permute-start | bytes 49160 | tf_op jit(solution)/shard_map/ppermute | solution.py:499
  103.6 5.8 %collective-permute-start.13 = (f32[8,512]{1,0:T(8,128)S(1)}, f32[8,512]{1,0:T(8,128)S(1)}, u32[]{:S(2)}, u32[]{:S(2)}) collective-permute-start(f32[8,512]{1,0:T(8,128)S(1)} %get-tuple-element.46), channel_id=1, source_target_pairs={{0,6},{1,7},{2,4},{3,5},{4,2},{5,3},{6,0},{7,1},{8,14},{9,15},{10,... | collective-permute-start | bytes 49160 | tf_op jit(solution)/shard_map/ppermute | solution.py:499

commit v2 on v1

--- a/solution.py
+++ b/solution.py
@@ -125,7 +125,8 @@
     )(q, g, o, k, v)
 
 
-def unpack_kernel(back_ref, q_ref, k_ref, v_ref, sems):
+def unpack_kernel(place_ref, back_ref, *refs):
+    parts, (q_ref, k_ref, v_ref, prompt_k_ref, prompt_v_ref, sems) = refs[:-6], refs[-6:]
     copies = []
     for h in range(KV_HEADS):
         thin = slice(h * HEAD_DIM, (h + 1) * HEAD_DIM)
@@ -133,25 +134,35 @@
         copies.append((back_ref.at[h, :, 0:QW], q_ref.at[:, wide]))
         copies.append((back_ref.at[h, :, QW : QW + HEAD_DIM], k_ref.at[:, thin]))
         copies.append((back_ref.at[h, :, QW + HEAD_DIM :], v_ref.at[:, thin]))
-    for copy in start_all(copies, sems):
+    copies = start_all(copies, sems)
+    for d, part in enumerate(parts):
+        for low in range(2):
+            cols = pl.ds(times(((place_ref[2] // 2) ^ d) * 2 + low, HEAD_DIM), HEAD_DIM)
+            at = 2 * low * HEAD_DIM
+            prompt_k_ref[:, cols] = part[:, at : at + HEAD_DIM].astype(BF16)
+            prompt_v_ref[:, cols] = part[:, at + HEAD_DIM : at + 2 * HEAD_DIM].astype(BF16)
+    for copy in copies:
         copy.wait()
 
 
-def unpack(back):
+def unpack(place, back, parts):
     rows = back.shape[1]
+    prompt = jax.ShapeDtypeStruct((parts[0].shape[0], KV_HEADS * HEAD_DIM), BF16)
     return pl.pallas_call(
         unpack_kernel,
-        in_specs=[ANY],
-        out_specs=[ANY] * 3,
+        in_specs=[SMEM, ANY] + [VMEM] * len(parts),
+        out_specs=[ANY] * 3 + [VMEM] * 2,
         out_shape=[
             jax.ShapeDtypeStruct((rows, KV_HEADS * QW), BF16),
             jax.ShapeDtypeStruct((rows, KV_HEADS * HEAD_DIM), BF16),
             jax.ShapeDtypeStruct((rows, KV_HEADS * HEAD_DIM), BF16),
+            prompt,
+            prompt,
         ],
         scratch_shapes=[pltpu.SemaphoreType.DMA((3 * KV_HEADS,))],
         compiler_params=params(4),
         name="unpack",
-    )(back)
+    )(place, back, *parts)
 
 
 def attend_kernel(place_ref, x_ref, pkv_low, pkv_high, back_out, *refs):
@@ -473,28 +484,6 @@
     )(place, *parts)
 
 
-def spread_kernel(place_ref, *refs):
-    parts, (k_ref, v_ref) = refs[:-2], refs[-2:]
-    for d, part in enumerate(parts):
-        for low in range(2):
-            cols = pl.ds(times(((place_ref[2] // 2) ^ d) * 2 + low, HEAD_DIM), HEAD_DIM)
-            at = 2 * low * HEAD_DIM
-            k_ref[:, cols] = part[:, at : at + HEAD_DIM].astype(BF16)
-            v_ref[:, cols] = part[:, at + HEAD_DIM : at + 2 * HEAD_DIM].astype(BF16)
-
-
-def spread_heads(place, parts):
-    shape = jax.ShapeDtypeStruct((parts[0].shape[0], KV_HEADS * HEAD_DIM), BF16)
-    return pl.pallas_call(
-        spread_kernel,
-        in_specs=[SMEM] + [VMEM] * len(parts),
-        out_specs=[VMEM] * 2,
-        out_shape=[shape] * 2,
-        compiler_params=params(4),
-        name="spread_heads",
-    )(place, *parts)
-
-
 def swap(value, axis, d):
     return lax.ppermute(value, axis, [(i, i ^ d) for i in range(lax.axis_size(axis))])
 
@@ -538,9 +527,8 @@
     keep, give = sum_over_x(place, parts)
     parts = sum_over_cores(place, keep, swap(give, "prefix", CORE_BIT))
     parts = sum_over_z(place, swap_all(parts, "prefix", 2 * X_BIT))
-    total = spread_heads(place, swap_all(parts, "resp", 2))
-    grad_query, grad_keys, grad_values = unpack(back)
-    return (grad_query[None], grad_keys[None], grad_values[None], total[0], total[1])
+    outs = unpack(place, back, swap_all(parts, "resp", 2))
+    return (*(out[None] for out in outs[:3]), outs[3], outs[4])
 
 
 def solution(mesh):

time: 112 us -> 114 us (1.018)
  starting transfers between devices: 32.3 us -> 39.9 us
  Pallas kernels: 38.1 us -> 30.8 us
    ppermute x12, starting transfers between devices: 16.5 us -> 26.2 us  [swap(): lax.ppermute(value, axis, [(i, i ^ d) for i in range(lax.axis_size(axis))])]
    pallas_call x1, Pallas kernels: 29.5 us -> 22.1 us  [attend(): pl.pallas_call(attend_kernel, in_specs=[SMEM, VMEM, ANY, ANY], out_specs=...]
    ppermute x2, starting transfers between devices: 6.56 us -> 4.54 us  [swap_across(): return lax.ppermute(value, ('prefix', 'resp'), pairs)]
    pallas_call x2 -> x1, Pallas kernels: 2.59 us -> 2.57 us  [unpack(): pl.pallas_call(unpack_kernel, in_specs=[SMEM, ANY] + [VMEM] * len(parts),...]
  transfers between devices with their start and end apart: 16 -> 16, of which waited for: 12 -> 12; matrix products, arithmetic and copies ran while one was open for 1% -> 1% of each run, Pallas kernels for 3% -> 2%
where the time goes in v2:
time: 114 us; the launch traced here: 113 us
  waiting for transfers between devices  40.2 us (35%)
  starting transfers between devices  39.9 us (35%)
  Pallas kernels  30.8 us (27%)
  between operations  1.56 us (1%)
    ppermute x12, starting transfers between devices, swap(): lax.ppermute(value, axis, [(i, i ^ d) for i in range(lax.axis_size(axis))])  26.2 us
    pallas_call x1, Pallas kernels, attend(): pl.pallas_call(attend_kernel, in_specs=[SMEM, VMEM, ANY, ANY], out_specs=...  22.1 us
    ppermute x12, waiting for transfers between devices, swap(): lax.ppermute(value, axis, [(i, i ^ d) for i in range(lax.axis_size(axis))])  21.3 us
    all_to_all x1, waiting for transfers between devices, local(): x = lax.all_to_all(send, 'resp', 0, 0, tiled=True)  15.6 us
    all_to_all x1, starting transfers between devices, local(): x = lax.all_to_all(send, 'resp', 0, 0, tiled=True)  5.49 us
    ppermute x2, starting transfers between devices, swap_across(): return lax.ppermute(value, ('prefix', 'resp'), pairs)  4.54 us
    pallas_call x1, Pallas kernels, pack(): pl.pallas_call(pack_kernel, in_specs=[HBM] * 5, out_specs=HBM, out_shape=...  4.27 us
    all_to_all x1, starting transfers between devices, local(): lax.all_to_all(back.reshape(KV_HEADS, rows, BACK_W), 'resp', 0, 0, tiled=...  3.72 us
  transfers between devices with their start and end apart: 16, of which 12 were waited for; matrix products, arithmetic and copies ran while one was open for 1% of the time, Pallas kernels for 2%

profile of v2, /device:TPU:0, one launch (start us, length us, event | category | flops | bytes accessed | tf_op | source)
XLA Modules:
  0.0 113.3 jit_solution(920333241242691869)
XLA Ops:
  0.6 4.3 %pack.1 = bf16[8,1552,128]{2,1,0:T(8,128)(2,1)} custom-call(bf16[128,5120]{1,0:T(8,128)(2,1)} %bitcast.16, bf16[128,5120]{1,0:T(8,128)(2,1)} %bitcast.17, bf16[128,5120]{1,0:T(8,128)(2,1)} %bitcast.18, bf16[128,1024]{1,0:T(8,128)(2,1)} %bitcast.19, bf16[128,1024]{1,0:T(8,128)(2,1)} %bitcast.20), custom_call_target="tpu_custom_call" | custom-call | tf_op jit(solution)/shard_map/pack/pallas_call | solution.py:111
  4.9 5.5 %all-to-all-start = ((bf16[8,1552,128]{2,1,0:T(8,128)(2,1)}), bf16[8,1552,128]{2,1,0:T(8,128)(2,1)S(1)}, u32[]{:S(2)}, u32[]{:S(2)}) async-start(bf16[8,1552,128]{2,1,0:T(8,128)(2,1)} %pack.1), calls=%async_computation | async-start | bytes 6356992 | tf_op jit(solution)/shard_map/all_to_all | solution.py:515
  11.2 3.4 %collective-permute-start = (bf16[1,64,256]{2,1,0:T(8,128)(2,1)S(1)}, bf16[1,64,256]{2,1,0:T(8,128)(2,1)S(1)}, u32[]{:S(2)}, u32[]{:S(2)}) collective-permute-start(bf16[1,64,256]{2,1,0:T(8,128)(2,1)S(1)} %maximum_bitcast_fusion.1), channel_id=1, source_target_pairs={{0,17},{1,16},{2,19},{3,18},{4,21},{5,20},{6,23},{7,22},{8,25},{9,... | collective-permute-start | bytes 98312 | tf_op jit(solution)/shard_map/ppermute | solution.py:498
  14.6 1.9 %collective-permute-done = bf16[1,64,256]{2,1,0:T(8,128)(2,1)S(1)} collective-permute-done((bf16[1,64,256]{2,1,0:T(8,128)(2,1)S(1)}, bf16[1,64,256]{2,1,0:T(8,128)(2,1)S(1)}, u32[]{:S(2)}, u32[]{:S(2)}) %collective-permute-start) | collective-permute-done | bytes 32800 | tf_op jit(solution)/shard_map/ppermute | solution.py:498
  16.6 1.2 %collective-permute-done.1 = bf16[2,64,256]{2,1,0:T(8,128)(2,1)S(1)} collective-permute-done((bf16[2,64,256]{2,1,0:T(8,128)(2,1)S(1)}, bf16[2,64,256]{2,1,0:T(8,128)(2,1)S(1)}, u32[]{:S(2)}, u32[]{:S(2)}) %collective-permute-start.1) | collective-permute-done | bytes 65568 | tf_op jit(solution)/shard_map/ppermute | solution.py:488
  17.8 2.0 %collective-permute-start.2 = (bf16[4,64,256]{2,1,0:T(8,128)(2,1)S(1)}, bf16[4,64,256]{2,1,0:T(8,128)(2,1)S(1)}, u32[]{:S(2)}, u32[]{:S(2)}) collective-permute-start(bf16[4,64,256]{2,1,0:T(8,128)(2,1)S(1)} %pad_maximum_fusion.1), channel_id=1, source_target_pairs={{0,32},{8,40},{16,48},{24,56},{32,0},{40,8},{48,16},{56,24},{64,96... | collective-permute-start | bytes 393224 | tf_op jit(solution)/shard_map/ppermute | solution.py:488
  19.8 3.8 %collective-permute-done.2 = bf16[4,64,256]{2,1,0:T(8,128)(2,1)S(1)} collective-permute-done((bf16[4,64,256]{2,1,0:T(8,128)(2,1)S(1)}, bf16[4,64,256]{2,1,0:T(8,128)(2,1)S(1)}, u32[]{:S(2)}, u32[]{:S(2)}) %collective-permute-start.2) | collective-permute-done | bytes 131104 | tf_op jit(solution)/shard_map/ppermute | solution.py:488
  23.7 3.8 %collective-permute-start.3 = (bf16[8,64,256]{2,1,0:T(8,128)(2,1)S(1)}, bf16[8,64,256]{2,1,0:T(8,128)(2,1)}, u32[]{:S(2)}, u32[]{:S(2)}) collective-permute-start(bf16[8,64,256]{2,1,0:T(8,128)(2,1)S(1)} %pad_maximum_fusion.pkv_low), channel_id=1, source_target_pairs={{0,64},{8,72},{16,80},{24,88},{32,96},{40,104},{48,112},{56,120},{... | collective-permute-start | bytes 786440 | tf_op jit(solution)/shard_map/ppermute | solution.py:488
  28.2 5.2 %collective-permute-done.3.pkv_high = bf16[8,64,256]{2,1,0:T(8,128)(2,1)} collective-permute-done((bf16[8,64,256]{2,1,0:T(8,128)(2,1)S(1)}, bf16[8,64,256]{2,1,0:T(8,128)(2,1)}, u32[]{:S(2)}, u32[]{:S(2)}) %collective-permute-start.3) | collective-permute-done | bytes 262176 | tf_op jit(solution)/shard_map/ppermute | solution.py:488
  33.4 15.6 %all-to-all-done.x_ref = bf16[8,1552,128]{2,1,0:T(8,128)(2,1)S(1)} async-done(((bf16[8,1552,128]{2,1,0:T(8,128)(2,1)}), bf16[8,1552,128]{2,1,0:T(8,128)(2,1)S(1)}, u32[]{:S(2)}, u32[]{:S(2)}) %all-to-all-start) | async-done | bytes 3178528 | tf_op jit(solution)/shard_map/all_to_all | solution.py:515
  49.0 22.1 %attend.1 = (bf16[1024,896]{1,0:T(8,128)(2,1)}, bf16[8,32,256]{2,1,0:T(8,128)(2,1)}, bf16[8,32,256]{2,1,0:T(8,128)(2,1)}, bf16[8,32,256]{2,1,0:T(8,128)(2,1)}, bf16[8,32,256]{2,1,0:T(8,128)(2,1)}) custom-call(s32[3]{0:T(128)S(1)} %pad_add_fusion.place_ref, bf16[8,1552,128]{2,1,0:T(8,128)(2,1)S(1)} %all-to-all-done.x_ref, ...), custom_call_target="tpu_custom_call" | custom-call | flops 13421772800 | bytes 5242880 | tf_op jit(solution)/shard_map/attend/pallas_call | solution.py:387
  71.1 2.8 %collective-permute-start.4 = (bf16[8,32,256]{2,1,0:T(8,128)(2,1)}, bf16[8,32,256]{2,1,0:T(8,128)(2,1)S(1)}, u32[]{:S(2)}, u32[]{:S(2)}) collective-permute-start(bf16[8,32,256]{2,1,0:T(8,128)(2,1)} %get-tuple-element.31), channel_id=1, source_target_pairs={{0,16},{8,24},{16,0},{24,8},{32,48},{40,56},{48,32},{56,40},{64,80... | collective-permute-start | bytes 393224 | tf_op jit(solution)/shard_map/ppermute | solution.py:488
  75.3 3.7 %all-to-all-start.1 = ((bf16[8,128,896]{2,1,0:T(8,128)(2,1)}), bf16[8,128,896]{2,1,0:T(8,128)(2,1)S(1)}, u32[]{:S(2)}, u32[]{:S(2)}) async-start(bf16[8,128,896]{2,1,0:T(8,128)(2,1)} %bitcast.15), calls=%async_computation.1 | async-start | bytes 3670016 | tf_op jit(solution)/shard_map/all_to_all | solution.py:525
  79.1 1.4 %collective-permute-done.6.both_ref = bf16[8,32,256]{2,1,0:T(8,128)(2,1)S(1)} collective-permute-done((bf16[8,32,256]{2,1,0:T(8,128)(2,1)}, bf16[8,32,256]{2,1,0:T(8,128)(2,1)S(1)}, u32[]{:S(2)}, u32[]{:S(2)}) %collective-permute-start.6) | collective-permute-done | bytes 131104 | tf_op jit(solution)/shard_map/ppermute | solution.py:498
  81.2 5.7 %collective-permute-start.7 = (f32[4,32,512]{2,1,0:T(8,128)S(1)}, f32[4,32,512]{2,1,0:T(8,128)S(1)}, u32[]{:S(2)}, u32[]{:S(2)}) collective-permute-start(f32[4,32,512]{2,1,0:T(8,128)S(1)} %get-tuple-element.35), channel_id=1, source_target_pairs={{0,8},{8,0},{16,24},{24,16},{32,40},{40,32},{48,56},{56,48},{64,72... | collective-permute-start | bytes 786440 | tf_op jit(solution)/shard_map/ppermute | solution.py:488
  88.6 2.0 %collective-permute-start.8 = (f32[32,512]{1,0:T(8,128)S(1)}, f32[32,512]{1,0:T(8,128)S(1)}, u32[]{:S(2)}, u32[]{:S(2)}) collective-permute-start(f32[32,512]{1,0:T(8,128)S(1)} %get-tuple-element.37), channel_id=1, source_target_pairs={{0,32},{8,40},{16,48},{24,56},{32,0},{40,8},{48,16},{56,24},{64,96... | collective-permute-start | bytes 196616 | tf_op jit(solution)/shard_map/ppermute | solution.py:488
  90.6 4.8 %collective-permute-start.9 = (f32[32,512]{1,0:T(8,128)S(1)}, f32[32,512]{1,0:T(8,128)S(1)}, u32[]{:S(2)}, u32[]{:S(2)}) collective-permute-start(f32[32,512]{1,0:T(8,128)S(1)} %get-tuple-element.38), channel_id=1, source_target_pairs={{0,64},{8,72},{16,80},{24,88},{32,96},{40,104},{48,112},{56,120},{... | collective-permute-start | bytes 196616 | tf_op jit(solution)/shard_map/ppermute | solution.py:488
  95.4 3.5 %collective-permute-done.9.refs_2_ = f32[32,512]{1,0:T(8,128)S(1)} collective-permute-done((f32[32,512]{1,0:T(8,128)S(1)}, f32[32,512]{1,0:T(8,128)S(1)}, u32[]{:S(2)}, u32[]{:S(2)}) %collective-permute-start.9) | collective-permute-done | bytes 65568 | tf_op jit(solution)/shard_map/ppermute | solution.py:488
  99.0 2.0 %collective-permute-done.10.refs_3_ = f32[32,512]{1,0:T(8,128)S(1)} collective-permute-done((f32[32,512]{1,0:T(8,128)S(1)}, f32[32,512]{1,0:T(8,128)S(1)}, u32[]{:S(2)}, u32[]{:S(2)}) %collective-permute-start.10) | collective-permute-done | bytes 65568 | tf_op jit(solution)/shard_map/ppermute | solution.py:488
  101.5 1.4 %collective-permute-start.11 = (f32[8,512]{1,0:T(8,128)S(1)}, f32[8,512]{1,0:T(8,128)S(1)}, u32[]{:S(2)}, u32[]{:S(2)}) collective-permute-start(f32[8,512]{1,0:T(8,128)S(1)} %get-tuple-element.41), channel_id=1, source_target_pairs={{0,2},{1,3},{2,0},{3,1},{4,6},{5,7},{6,4},{7,5},{8,10},{9,11},{10,... | collective-permute-start | bytes 49160 | tf_op jit(solution)/shard_map/ppermute | solution.py:488
  102.9 2.7 %collective-permute-start.12 = (f32[8,512]{1,0:T(8,128)S(1)}, f32[8,512]{1,0:T(8,128)S(1)}, u32[]{:S(2)}, u32[]{:S(2)}) collective-permute-start(f32[8,512]{1,0:T(8,128)S(1)} %get-tuple-element.42), channel_id=1, source_target_pairs={{0,4},{1,5},{2,6},{3,7},{4,0},{5,1},{6,2},{7,3},{8,12},{9,13},{10,... | collective-permute-start | bytes 49160 | tf_op jit(solution)/shard_map/ppermute | solution.py:488
  106.3 1.9 %collective-permute-done.12.refs_2_ = f32[8,512]{1,0:T(8,128)S(1)} collective-permute-done((f32[8,512]{1,0:T(8,128)S(1)}, f32[8,512]{1,0:T(8,128)S(1)}, u32[]{:S(2)}, u32[]{:S(2)}) %collective-permute-start.12) | collective-permute-done | bytes 16416 | tf_op jit(solution)/shard_map/ppermute | solution.py:488
  108.2 2.4 %collective-permute-done.13.refs_3_ = f32[8,512]{1,0:T(8,128)S(1)} collective-permute-done((f32[8,512]{1,0:T(8,128)S(1)}, f32[8,512]{1,0:T(8,128)S(1)}, u32[]{:S(2)}, u32[]{:S(2)}) %collective-permute-start.13) | collective-permute-done | bytes 16416 | tf_op jit(solution)/shard_map/ppermute | solution.py:488
  110.6 2.6 %unpack.1 = (bf16[128,5120]{1,0:T(8,128)(2,1)}, bf16[128,1024]{1,0:T(8,128)(2,1)}, bf16[128,1024]{1,0:T(8,128)(2,1)}, bf16[8,1024]{1,0:T(8,128)(2,1)}, bf16[8,1024]{1,0:T(8,128)(2,1)}) custom-call(s32[3]{0:T(128)S(1)} %pad_add_fusion.place_ref, bf16[8,128,896]{2,1,0:T(8,128)(2,1)S(1)} %all-to-all-done.1.back_ref, f32[8,512]{1,0:T(8,128)S(1)} %get-tuple-element.40.refs_0_, ...), custom_call_target="tpu_custom_call" | custom-call | tf_op jit(solution)/shard_map/unpack/pallas_call | solution.py:151
  (23 shorter events, 6.0 us)
Async XLA Ops:
  4.9 44.1 %all-to-all-start = ((bf16[8,1552,128]{2,1,0:T(8,128)(2,1)}), bf16[8,1552,128]{2,1,0:T(8,128)(2,1)S(1)}, u32[]{:S(2)}, u32[]{:S(2)}) async-start(bf16[8,1552,128]{2,1,0:T(8,128)(2,1)} %pack.1), calls=%async_computation | async-start | bytes 6356992 | tf_op jit(solution)/shard_map/all_to_all | solution.py:515
  11.2 5.3 %collective-permute-start = (bf16[1,64,256]{2,1,0:T(8,128)(2,1)S(1)}, bf16[1,64,256]{2,1,0:T(8,128)(2,1)S(1)}, u32[]{:S(2)}, u32[]{:S(2)}) collective-permute-start(bf16[1,64,256]{2,1,0:T(8,128)(2,1)S(1)} %maximum_bitcast_fusion.1), channel_id=1, source_target_pairs={{0,17},{1,16},{2,19},{3,18},{4,21},{5,20},{6,23},{7,22},{8,25},{9,... | collective-permute-start | bytes 98312 | tf_op jit(solution)/shard_map/ppermute | solution.py:498
  16.5 1.3 %collective-permute-start.1 = (bf16[2,64,256]{2,1,0:T(8,128)(2,1)S(1)}, bf16[2,64,256]{2,1,0:T(8,128)(2,1)S(1)}, u32[]{:S(2)}, u32[]{:S(2)}) collective-permute-start(bf16[2,64,256]{2,1,0:T(8,128)(2,1)S(1)} %pad_maximum_fusion.2), channel_id=1, source_target_pairs={{0,8},{8,0},{16,24},{24,16},{32,40},{40,32},{48,56},{56,48},{64,72... | collective-permute-start | bytes 196616 | tf_op jit(solution)/shard_map/ppermute | solution.py:488
  17.8 5.8 %collective-permute-start.2 = (bf16[4,64,256]{2,1,0:T(8,128)(2,1)S(1)}, bf16[4,64,256]{2,1,0:T(8,128)(2,1)S(1)}, u32[]{:S(2)}, u32[]{:S(2)}) collective-permute-start(bf16[4,64,256]{2,1,0:T(8,128)(2,1)S(1)} %pad_maximum_fusion.1), channel_id=1, source_target_pairs={{0,32},{8,40},{16,48},{24,56},{32,0},{40,8},{48,16},{56,24},{64,96... | collective-permute-start | bytes 393224 | tf_op jit(solution)/shard_map/ppermute | solution.py:488
  23.7 9.7 %collective-permute-start.3 = (bf16[8,64,256]{2,1,0:T(8,128)(2,1)S(1)}, bf16[8,64,256]{2,1,0:T(8,128)(2,1)}, u32[]{:S(2)}, u32[]{:S(2)}) collective-permute-start(bf16[8,64,256]{2,1,0:T(8,128)(2,1)S(1)} %pad_maximum_fusion.pkv_low), channel_id=1, source_target_pairs={{0,64},{8,72},{16,80},{24,88},{32,96},{40,104},{48,112},{56,120},{... | collective-permute-start | bytes 786440 | tf_op jit(solution)/shard_map/ppermute | solution.py:488
  71.1 7.9 %collective-permute-start.4 = (bf16[8,32,256]{2,1,0:T(8,128)(2,1)}, bf16[8,32,256]{2,1,0:T(8,128)(2,1)S(1)}, u32[]{:S(2)}, u32[]{:S(2)}) collective-permute-start(bf16[8,32,256]{2,1,0:T(8,128)(2,1)} %get-tuple-element.31), channel_id=1, source_target_pairs={{0,16},{8,24},{16,0},{24,8},{32,48},{40,56},{48,32},{56,40},{64,80... | collective-permute-start | bytes 393224 | tf_op jit(solution)/shard_map/ppermute | solution.py:488
  73.9 5.2 %collective-permute-start.5 = (bf16[8,32,256]{2,1,0:T(8,128)(2,1)}, bf16[8,32,256]{2,1,0:T(8,128)(2,1)S(1)}, u32[]{:S(2)}, u32[]{:S(2)}) collective-permute-start(bf16[8,32,256]{2,1,0:T(8,128)(2,1)} %get-tuple-element.32), channel_id=1, source_target_pairs={{0,1},{1,0},{2,3},{3,2},{4,5},{5,4},{6,7},{7,6},{8,9},{9,8},{10,11... | collective-permute-start | bytes 393224 | tf_op jit(solution)/shard_map/ppermute | solution.py:488
  74.1 6.4 %collective-permute-start.6 = (bf16[8,32,256]{2,1,0:T(8,128)(2,1)}, bf16[8,32,256]{2,1,0:T(8,128)(2,1)S(1)}, u32[]{:S(2)}, u32[]{:S(2)}) collective-permute-start(bf16[8,32,256]{2,1,0:T(8,128)(2,1)} %get-tuple-element.33), channel_id=1, source_target_pairs={{0,17},{1,16},{2,19},{3,18},{4,21},{5,20},{6,23},{7,22},{8,25},{9,... | collective-permute-start | bytes 393224 | tf_op jit(solution)/shard_map/ppermute | solution.py:498
  75.3 5.2 %copy-start = (bf16[8,32,256]{2,1,0:T(8,128)(2,1)S(1)}, bf16[8,32,256]{2,1,0:T(8,128)(2,1)}, u32[]{:S(2)}) copy-start(bf16[8,32,256]{2,1,0:T(8,128)(2,1)} %get-tuple-element.30.mine_ref) | copy-start | bytes 393220
  75.3 35.3 %all-to-all-start.1 = ((bf16[8,128,896]{2,1,0:T(8,128)(2,1)}), bf16[8,128,896]{2,1,0:T(8,128)(2,1)S(1)}, u32[]{:S(2)}, u32[]{:S(2)}) async-start(bf16[8,128,896]{2,1,0:T(8,128)(2,1)} %bitcast.15), calls=%async_computation.1 | async-start | bytes 3670016 | tf_op jit(solution)/shard_map/all_to_all | solution.py:525
  81.2 6.8 %collective-permute-start.7 = (f32[4,32,512]{2,1,0:T(8,128)S(1)}, f32[4,32,512]{2,1,0:T(8,128)S(1)}, u32[]{:S(2)}, u32[]{:S(2)}) collective-permute-start(f32[4,32,512]{2,1,0:T(8,128)S(1)} %get-tuple-element.35), channel_id=1, source_target_pairs={{0,8},{8,0},{16,24},{24,16},{32,40},{40,32},{48,56},{56,48},{64,72... | collective-permute-start | bytes 786440 | tf_op jit(solution)/shard_map/ppermute | solution.py:488
  88.6 6.8 %collective-permute-start.8 = (f32[32,512]{1,0:T(8,128)S(1)}, f32[32,512]{1,0:T(8,128)S(1)}, u32[]{:S(2)}, u32[]{:S(2)}) collective-permute-start(f32[32,512]{1,0:T(8,128)S(1)} %get-tuple-element.37), channel_id=1, source_target_pairs={{0,32},{8,40},{16,48},{24,56},{32,0},{40,8},{48,16},{56,24},{64,96... | collective-permute-start | bytes 196616 | tf_op jit(solution)/shard_map/ppermute | solution.py:488
  90.6 8.4 %collective-permute-start.9 = (f32[32,512]{1,0:T(8,128)S(1)}, f32[32,512]{1,0:T(8,128)S(1)}, u32[]{:S(2)}, u32[]{:S(2)}) collective-permute-start(f32[32,512]{1,0:T(8,128)S(1)} %get-tuple-element.38), channel_id=1, source_target_pairs={{0,64},{8,72},{16,80},{24,88},{32,96},{40,104},{48,112},{56,120},{... | collective-permute-start | bytes 196616 | tf_op jit(solution)/shard_map/ppermute | solution.py:488
  95.4 5.5 %collective-permute-start.10 = (f32[32,512]{1,0:T(8,128)S(1)}, f32[32,512]{1,0:T(8,128)S(1)}, u32[]{:S(2)}, u32[]{:S(2)}) collective-permute-start(f32[32,512]{1,0:T(8,128)S(1)} %get-tuple-element.39), channel_id=1, source_target_pairs={{0,96},{8,104},{16,112},{24,120},{32,64},{40,72},{48,80},{56,88},{... | collective-permute-start | bytes 196616 | tf_op jit(solution)/shard_map/ppermute | solution.py:488
  101.5 4.8 %collective-permute-start.11 = (f32[8,512]{1,0:T(8,128)S(1)}, f32[8,512]{1,0:T(8,128)S(1)}, u32[]{:S(2)}, u32[]{:S(2)}) collective-permute-start(f32[8,512]{1,0:T(8,128)S(1)} %get-tuple-element.41), channel_id=1, source_target_pairs={{0,2},{1,3},{2,0},{3,1},{4,6},{5,7},{6,4},{7,5},{8,10},{9,11},{10,... | collective-permute-start | bytes 49160 | tf_op jit(solution)/shard_map/ppermute | solution.py:488
  102.9 5.2 %collective-permute-start.12 = (f32[8,512]{1,0:T(8,128)S(1)}, f32[8,512]{1,0:T(8,128)S(1)}, u32[]{:S(2)}, u32[]{:S(2)}) collective-permute-start(f32[8,512]{1,0:T(8,128)S(1)} %get-tuple-element.42), channel_id=1, source_target_pairs={{0,4},{1,5},{2,6},{3,7},{4,0},{5,1},{6,2},{7,3},{8,12},{9,13},{10,... | collective-permute-start | bytes 49160 | tf_op jit(solution)/shard_map/ppermute | solution.py:488
  105.6 4.9 %collective-permute-start.13 = (f32[8,512]{1,0:T(8,128)S(1)}, f32[8,512]{1,0:T(8,128)S(1)}, u32[]{:S(2)}, u32[]{:S(2)}) collective-permute-start(f32[8,512]{1,0:T(8,128)S(1)} %get-tuple-element.43), channel_id=1, source_target_pairs={{0,6},{1,7},{2,4},{3,5},{4,2},{5,3},{6,0},{7,1},{8,14},{9,15},{10,... | collective-permute-start | bytes 49160 | tf_op jit(solution)/shard_map/ppermute | solution.py:488

commit v3 on v2

--- a/solution.py
+++ b/solution.py
@@ -15,7 +15,7 @@
 TILE = 256
 STATS = 16
 UNSEEN = -1e30
-PACK_ROWS = 32
+PACK_ROWS = 16
 GATHER_BITS = (1, 0, 2, 3)
 COLUMNS = 2 + 2 * GROUP
 DELTA_ROWS = 16

time: 114 us -> 114 us (level)
  Pallas kernels: 30.8 us -> 38.5 us
  starting transfers between devices: 39.9 us -> 33 us
  waiting for transfers between devices: 40.2 us -> 38.3 us
    ppermute x12, starting transfers between devices: 26.2 us -> 17.2 us  [swap(): lax.ppermute(value, axis, [(i, i ^ d) for i in range(lax.axis_size(axis))])]
    pallas_call x1, Pallas kernels: 22.1 us -> 29.5 us  [attend(): pl.pallas_call(attend_kernel, in_specs=[SMEM, VMEM, ANY, ANY], out_specs=...]
    ppermute x2, starting transfers between devices: 4.54 us -> 6.55 us  [swap_across(): return lax.ppermute(value, ('prefix', 'resp'), pairs)]
    ppermute x12, waiting for transfers between devices: 21.3 us -> 20.1 us  [swap(): lax.ppermute(value, axis, [(i, i ^ d) for i in range(lax.axis_size(axis))])]
where the time goes in v3:
time: 114 us; the launch traced here: 112 us
  Pallas kernels  38.5 us (34%)
  waiting for transfers between devices  38.3 us (34%)
  starting transfers between devices  33 us (29%)
  between operations  1.58 us (1%)
    pallas_call x1, Pallas kernels, attend(): pl.pallas_call(attend_kernel, in_specs=[SMEM, VMEM, ANY, ANY], out_specs=...  29.5 us
    ppermute x12, waiting for transfers between devices, swap(): lax.ppermute(value, axis, [(i, i ^ d) for i in range(lax.axis_size(axis))])  20.1 us
    ppermute x12, starting transfers between devices, swap(): lax.ppermute(value, axis, [(i, i ^ d) for i in range(lax.axis_size(axis))])  17.2 us
    all_to_all x1, waiting for transfers between devices, local(): x = lax.all_to_all(send, 'resp', 0, 0, tiled=True)  15.6 us
    ppermute x2, starting transfers between devices, swap_across(): return lax.ppermute(value, ('prefix', 'resp'), pairs)  6.55 us
    all_to_all x1, starting transfers between devices, local(): x = lax.all_to_all(send, 'resp', 0, 0, tiled=True)  5.49 us
    pallas_call x1, Pallas kernels, pack(): pl.pallas_call(pack_kernel, in_specs=[HBM] * 5, out_specs=HBM, out_shape=...  4.64 us
    all_to_all x1, starting transfers between devices, local(): lax.all_to_all(back.reshape(KV_HEADS, rows, BACK_W), 'resp', 0, 0, tiled=...  3.72 us
  transfers between devices with their start and end apart: 16, of which 12 were waited for; matrix products, arithmetic and copies ran while one was open for 1% of the time, Pallas kernels for 2%

profile of v3, /device:TPU:0, one launch (start us, length us, event | category | flops | bytes accessed | tf_op | source)
XLA Modules:
  0.0 112.4 jit_solution(264647630466304291)
XLA Ops:
  0.6 4.6 %pack.1 = bf16[8,1552,128]{2,1,0:T(8,128)(2,1)} custom-call(bf16[128,5120]{1,0:T(8,128)(2,1)} %bitcast.16, bf16[128,5120]{1,0:T(8,128)(2,1)} %bitcast.17, bf16[128,5120]{1,0:T(8,128)(2,1)} %bitcast.18, bf16[128,1024]{1,0:T(8,128)(2,1)} %bitcast.19, bf16[128,1024]{1,0:T(8,128)(2,1)} %bitcast.20), custom_call_target="tpu_custom_call" | custom-call | tf_op jit(solution)/shard_map/pack/pallas_call | solution.py:111
  5.3 5.5 %all-to-all-start = ((bf16[8,1552,128]{2,1,0:T(8,128)(2,1)}), bf16[8,1552,128]{2,1,0:T(8,128)(2,1)S(1)}, u32[]{:S(2)}, u32[]{:S(2)}) async-start(bf16[8,1552,128]{2,1,0:T(8,128)(2,1)} %pack.1), calls=%async_computation | async-start | bytes 6356992 | tf_op jit(solution)/shard_map/all_to_all | solution.py:515
  11.6 3.4 %collective-permute-start = (bf16[1,64,256]{2,1,0:T(8,128)(2,1)S(1)}, bf16[1,64,256]{2,1,0:T(8,128)(2,1)S(1)}, u32[]{:S(2)}, u32[]{:S(2)}) collective-permute-start(bf16[1,64,256]{2,1,0:T(8,128)(2,1)S(1)} %maximum_bitcast_fusion.1), channel_id=1, source_target_pairs={{0,17},{1,16},{2,19},{3,18},{4,21},{5,20},{6,23},{7,22},{8,25},{9,... | collective-permute-start | bytes 98312 | tf_op jit(solution)/shard_map/ppermute | solution.py:498
  14.9 1.9 %collective-permute-done = bf16[1,64,256]{2,1,0:T(8,128)(2,1)S(1)} collective-permute-done((bf16[1,64,256]{2,1,0:T(8,128)(2,1)S(1)}, bf16[1,64,256]{2,1,0:T(8,128)(2,1)S(1)}, u32[]{:S(2)}, u32[]{:S(2)}) %collective-permute-start) | collective-permute-done | bytes 32800 | tf_op jit(solution)/shard_map/ppermute | solution.py:498
  16.9 1.2 %collective-permute-done.1 = bf16[2,64,256]{2,1,0:T(8,128)(2,1)S(1)} collective-permute-done((bf16[2,64,256]{2,1,0:T(8,128)(2,1)S(1)}, bf16[2,64,256]{2,1,0:T(8,128)(2,1)S(1)}, u32[]{:S(2)}, u32[]{:S(2)}) %collective-permute-start.1) | collective-permute-done | bytes 65568 | tf_op jit(solution)/shard_map/ppermute | solution.py:488
  18.2 2.0 %collective-permute-start.2 = (bf16[4,64,256]{2,1,0:T(8,128)(2,1)S(1)}, bf16[4,64,256]{2,1,0:T(8,128)(2,1)S(1)}, u32[]{:S(2)}, u32[]{:S(2)}) collective-permute-start(bf16[4,64,256]{2,1,0:T(8,128)(2,1)S(1)} %pad_maximum_fusion.1), channel_id=1, source_target_pairs={{0,32},{8,40},{16,48},{24,56},{32,0},{40,8},{48,16},{56,24},{64,96... | collective-permute-start | bytes 393224 | tf_op jit(solution)/shard_map/ppermute | solution.py:488
  20.2 3.8 %collective-permute-done.2 = bf16[4,64,256]{2,1,0:T(8,128)(2,1)S(1)} collective-permute-done((bf16[4,64,256]{2,1,0:T(8,128)(2,1)S(1)}, bf16[4,64,256]{2,1,0:T(8,128)(2,1)S(1)}, u32[]{:S(2)}, u32[]{:S(2)}) %collective-permute-start.2) | collective-permute-done | bytes 131104 | tf_op jit(solution)/shard_map/ppermute | solution.py:488
  24.0 3.8 %collective-permute-start.3 = (bf16[8,64,256]{2,1,0:T(8,128)(2,1)S(1)}, bf16[8,64,256]{2,1,0:T(8,128)(2,1)}, u32[]{:S(2)}, u32[]{:S(2)}) collective-permute-start(bf16[8,64,256]{2,1,0:T(8,128)(2,1)S(1)} %pad_maximum_fusion.pkv_low), channel_id=1, source_target_pairs={{0,64},{8,72},{16,80},{24,88},{32,96},{40,104},{48,112},{56,120},{... | collective-permute-start | bytes 786440 | tf_op jit(solution)/shard_map/ppermute | solution.py:488
  28.5 5.2 %collective-permute-done.3.pkv_high = bf16[8,64,256]{2,1,0:T(8,128)(2,1)} collective-permute-done((bf16[8,64,256]{2,1,0:T(8,128)(2,1)S(1)}, bf16[8,64,256]{2,1,0:T(8,128)(2,1)}, u32[]{:S(2)}, u32[]{:S(2)}) %collective-permute-start.3) | collective-permute-done | bytes 262176 | tf_op jit(solution)/shard_map/ppermute | solution.py:488
  33.7 15.6 %all-to-all-done.x_ref = bf16[8,1552,128]{2,1,0:T(8,128)(2,1)S(1)} async-done(((bf16[8,1552,128]{2,1,0:T(8,128)(2,1)}), bf16[8,1552,128]{2,1,0:T(8,128)(2,1)S(1)}, u32[]{:S(2)}, u32[]{:S(2)}) %all-to-all-start) | async-done | bytes 3178528 | tf_op jit(solution)/shard_map/all_to_all | solution.py:515
  49.3 29.5 %attend.1 = (bf16[1024,896]{1,0:T(8,128)(2,1)}, bf16[8,32,256]{2,1,0:T(8,128)(2,1)}, bf16[8,32,256]{2,1,0:T(8,128)(2,1)}, bf16[8,32,256]{2,1,0:T(8,128)(2,1)}, bf16[8,32,256]{2,1,0:T(8,128)(2,1)}) custom-call(s32[3]{0:T(128)S(1)} %pad_add_fusion.place_ref, bf16[8,1552,128]{2,1,0:T(8,128)(2,1)S(1)} %all-to-all-done.x_ref, ...), custom_call_target="tpu_custom_call" | custom-call | flops 13421772800 | bytes 5242880 | tf_op jit(solution)/shard_map/attend/pallas_call | solution.py:387
  79.0 0.9 collective-permute-start.5
  79.9 3.2 %collective-permute-start.6 = (bf16[8,32,256]{2,1,0:T(8,128)(2,1)}, bf16[8,32,256]{2,1,0:T(8,128)(2,1)S(1)}, u32[]{:S(2)}, u32[]{:S(2)}) collective-permute-start(bf16[8,32,256]{2,1,0:T(8,128)(2,1)} %get-tuple-element.33), channel_id=1, source_target_pairs={{0,17},{1,16},{2,19},{3,18},{4,21},{5,20},{6,23},{7,22},{8,25},{9,... | collective-permute-start | bytes 393224 | tf_op jit(solution)/shard_map/ppermute | solution.py:498
  83.0 3.7 %all-to-all-start.1 = ((bf16[8,128,896]{2,1,0:T(8,128)(2,1)}), bf16[8,128,896]{2,1,0:T(8,128)(2,1)S(1)}, u32[]{:S(2)}, u32[]{:S(2)}) async-start(bf16[8,128,896]{2,1,0:T(8,128)(2,1)} %bitcast.15), calls=%async_computation.1 | async-start | bytes 3670016 | tf_op jit(solution)/shard_map/all_to_all | solution.py:525
  88.3 1.5 %collective-permute-done.7.got_ref = f32[4,32,512]{2,1,0:T(8,128)S(1)} collective-permute-done((f32[4,32,512]{2,1,0:T(8,128)S(1)}, f32[4,32,512]{2,1,0:T(8,128)S(1)}, u32[]{:S(2)}, u32[]{:S(2)}) %collective-permute-start.7) | collective-permute-done | bytes 262176 | tf_op jit(solution)/shard_map/ppermute | solution.py:488
  90.4 2.8 %collective-permute-start.8 = (f32[32,512]{1,0:T(8,128)S(1)}, f32[32,512]{1,0:T(8,128)S(1)}, u32[]{:S(2)}, u32[]{:S(2)}) collective-permute-start(f32[32,512]{1,0:T(8,128)S(1)} %get-tuple-element.37), channel_id=1, source_target_pairs={{0,32},{8,40},{16,48},{24,56},{32,0},{40,8},{48,16},{56,24},{64,96... | collective-permute-start | bytes 196616 | tf_op jit(solution)/shard_map/ppermute | solution.py:488
  93.1 2.8 %collective-permute-start.10 = (f32[32,512]{1,0:T(8,128)S(1)}, f32[32,512]{1,0:T(8,128)S(1)}, u32[]{:S(2)}, u32[]{:S(2)}) collective-permute-start(f32[32,512]{1,0:T(8,128)S(1)} %get-tuple-element.39), channel_id=1, source_target_pairs={{0,96},{8,104},{16,112},{24,120},{32,64},{40,72},{48,80},{56,88},{... | collective-permute-start | bytes 196616 | tf_op jit(solution)/shard_map/ppermute | solution.py:488
  96.0 2.9 %collective-permute-done.9.refs_2_ = f32[32,512]{1,0:T(8,128)S(1)} collective-permute-done((f32[32,512]{1,0:T(8,128)S(1)}, f32[32,512]{1,0:T(8,128)S(1)}, u32[]{:S(2)}, u32[]{:S(2)}) %collective-permute-start.9) | collective-permute-done | bytes 65568 | tf_op jit(solution)/shard_map/ppermute | solution.py:488
  100.2 0.9 collective-permute-start.11
  101.1 2.5 %collective-permute-start.12 = (f32[8,512]{1,0:T(8,128)S(1)}, f32[8,512]{1,0:T(8,128)S(1)}, u32[]{:S(2)}, u32[]{:S(2)}) collective-permute-start(f32[8,512]{1,0:T(8,128)S(1)} %get-tuple-element.42), channel_id=1, source_target_pairs={{0,4},{1,5},{2,6},{3,7},{4,0},{5,1},{6,2},{7,3},{8,12},{9,13},{10,... | collective-permute-start | bytes 49160 | tf_op jit(solution)/shard_map/ppermute | solution.py:488
  103.7 1.3 %collective-permute-start.13 = (f32[8,512]{1,0:T(8,128)S(1)}, f32[8,512]{1,0:T(8,128)S(1)}, u32[]{:S(2)}, u32[]{:S(2)}) collective-permute-start(f32[8,512]{1,0:T(8,128)S(1)} %get-tuple-element.43), channel_id=1, source_target_pairs={{0,6},{1,7},{2,4},{3,5},{4,2},{5,3},{6,0},{7,1},{8,14},{9,15},{10,... | collective-permute-start | bytes 49160 | tf_op jit(solution)/shard_map/ppermute | solution.py:488
  105.0 2.8 %collective-permute-done.11.refs_1_ = f32[8,512]{1,0:T(8,128)S(1)} collective-permute-done((f32[8,512]{1,0:T(8,128)S(1)}, f32[8,512]{1,0:T(8,128)S(1)}, u32[]{:S(2)}, u32[]{:S(2)}) %collective-permute-start.11) | collective-permute-done | bytes 16416 | tf_op jit(solution)/shard_map/ppermute | solution.py:488
  107.8 1.9 %collective-permute-done.13.refs_3_ = f32[8,512]{1,0:T(8,128)S(1)} collective-permute-done((f32[8,512]{1,0:T(8,128)S(1)}, f32[8,512]{1,0:T(8,128)S(1)}, u32[]{:S(2)}, u32[]{:S(2)}) %collective-permute-start.13) | collective-permute-done | bytes 16416 | tf_op jit(solution)/shard_map/ppermute | solution.py:488
  109.6 2.6 %unpack.1 = (bf16[128,5120]{1,0:T(8,128)(2,1)}, bf16[128,1024]{1,0:T(8,128)(2,1)}, bf16[128,1024]{1,0:T(8,128)(2,1)}, bf16[8,1024]{1,0:T(8,128)(2,1)}, bf16[8,1024]{1,0:T(8,128)(2,1)}) custom-call(s32[3]{0:T(128)S(1)} %pad_add_fusion.place_ref, bf16[8,128,896]{2,1,0:T(8,128)(2,1)S(1)} %all-to-all-done.1.back_ref, f32[8,512]{1,0:T(8,128)S(1)} %get-tuple-element.40.refs_0_, ...), custom_call_target="tpu_custom_call" | custom-call | tf_op jit(solution)/shard_map/unpack/pallas_call | solution.py:151
  (23 shorter events, 4.5 us)
Async XLA Ops:
  5.3 44.1 %all-to-all-start = ((bf16[8,1552,128]{2,1,0:T(8,128)(2,1)}), bf16[8,1552,128]{2,1,0:T(8,128)(2,1)S(1)}, u32[]{:S(2)}, u32[]{:S(2)}) async-start(bf16[8,1552,128]{2,1,0:T(8,128)(2,1)} %pack.1), calls=%async_computation | async-start | bytes 6356992 | tf_op jit(solution)/shard_map/all_to_all | solution.py:515
  11.6 5.3 %collective-permute-start = (bf16[1,64,256]{2,1,0:T(8,128)(2,1)S(1)}, bf16[1,64,256]{2,1,0:T(8,128)(2,1)S(1)}, u32[]{:S(2)}, u32[]{:S(2)}) collective-permute-start(bf16[1,64,256]{2,1,0:T(8,128)(2,1)S(1)} %maximum_bitcast_fusion.1), channel_id=1, source_target_pairs={{0,17},{1,16},{2,19},{3,18},{4,21},{5,20},{6,23},{7,22},{8,25},{9,... | collective-permute-start | bytes 98312 | tf_op jit(solution)/shard_map/ppermute | solution.py:498
  16.8 1.3 %collective-permute-start.1 = (bf16[2,64,256]{2,1,0:T(8,128)(2,1)S(1)}, bf16[2,64,256]{2,1,0:T(8,128)(2,1)S(1)}, u32[]{:S(2)}, u32[]{:S(2)}) collective-permute-start(bf16[2,64,256]{2,1,0:T(8,128)(2,1)S(1)} %pad_maximum_fusion.2), channel_id=1, source_target_pairs={{0,8},{8,0},{16,24},{24,16},{32,40},{40,32},{48,56},{56,48},{64,72... | collective-permute-start | bytes 196616 | tf_op jit(solution)/shard_map/ppermute | solution.py:488
  18.2 5.8 %collective-permute-start.2 = (bf16[4,64,256]{2,1,0:T(8,128)(2,1)S(1)}, bf16[4,64,256]{2,1,0:T(8,128)(2,1)S(1)}, u32[]{:S(2)}, u32[]{:S(2)}) collective-permute-start(bf16[4,64,256]{2,1,0:T(8,128)(2,1)S(1)} %pad_maximum_fusion.1), channel_id=1, source_target_pairs={{0,32},{8,40},{16,48},{24,56},{32,0},{40,8},{48,16},{56,24},{64,96... | collective-permute-start | bytes 393224 | tf_op jit(solution)/shard_map/ppermute | solution.py:488
  24.0 9.7 %collective-permute-start.3 = (bf16[8,64,256]{2,1,0:T(8,128)(2,1)S(1)}, bf16[8,64,256]{2,1,0:T(8,128)(2,1)}, u32[]{:S(2)}, u32[]{:S(2)}) collective-permute-start(bf16[8,64,256]{2,1,0:T(8,128)(2,1)S(1)} %pad_maximum_fusion.pkv_low), channel_id=1, source_target_pairs={{0,64},{8,72},{16,80},{24,88},{32,96},{40,104},{48,112},{56,120},{... | collective-permute-start | bytes 786440 | tf_op jit(solution)/shard_map/ppermute | solution.py:488
  78.9 7.9 %collective-permute-start.4 = (bf16[8,32,256]{2,1,0:T(8,128)(2,1)}, bf16[8,32,256]{2,1,0:T(8,128)(2,1)S(1)}, u32[]{:S(2)}, u32[]{:S(2)}) collective-permute-start(bf16[8,32,256]{2,1,0:T(8,128)(2,1)} %get-tuple-element.31), channel_id=1, source_target_pairs={{0,16},{8,24},{16,0},{24,8},{32,48},{40,56},{48,32},{56,40},{64,80... | collective-permute-start | bytes 393224 | tf_op jit(solution)/shard_map/ppermute | solution.py:488
  79.0 7.8 %collective-permute-start.5 = (bf16[8,32,256]{2,1,0:T(8,128)(2,1)}, bf16[8,32,256]{2,1,0:T(8,128)(2,1)S(1)}, u32[]{:S(2)}, u32[]{:S(2)}) collective-permute-start(bf16[8,32,256]{2,1,0:T(8,128)(2,1)} %get-tuple-element.32), channel_id=1, source_target_pairs={{0,1},{1,0},{2,3},{3,2},{4,5},{5,4},{6,7},{7,6},{8,9},{9,8},{10,11... | collective-permute-start | bytes 393224 | tf_op jit(solution)/shard_map/ppermute | solution.py:488
  79.9 7.7 %collective-permute-start.6 = (bf16[8,32,256]{2,1,0:T(8,128)(2,1)}, bf16[8,32,256]{2,1,0:T(8,128)(2,1)S(1)}, u32[]{:S(2)}, u32[]{:S(2)}) collective-permute-start(bf16[8,32,256]{2,1,0:T(8,128)(2,1)} %get-tuple-element.33), channel_id=1, source_target_pairs={{0,17},{1,16},{2,19},{3,18},{4,21},{5,20},{6,23},{7,22},{8,25},{9,... | collective-permute-start | bytes 393224 | tf_op jit(solution)/shard_map/ppermute | solution.py:498
  83.0 4.5 %copy-start = (bf16[8,32,256]{2,1,0:T(8,128)(2,1)S(1)}, bf16[8,32,256]{2,1,0:T(8,128)(2,1)}, u32[]{:S(2)}) copy-start(bf16[8,32,256]{2,1,0:T(8,128)(2,1)} %get-tuple-element.30.mine_ref) | copy-start | bytes 393220
  83.0 26.6 %all-to-all-start.1 = ((bf16[8,128,896]{2,1,0:T(8,128)(2,1)}), bf16[8,128,896]{2,1,0:T(8,128)(2,1)S(1)}, u32[]{:S(2)}, u32[]{:S(2)}) async-start(bf16[8,128,896]{2,1,0:T(8,128)(2,1)} %bitcast.15), calls=%async_computation.1 | async-start | bytes 3670016 | tf_op jit(solution)/shard_map/all_to_all | solution.py:525
  88.2 1.6 %collective-permute-start.7 = (f32[4,32,512]{2,1,0:T(8,128)S(1)}, f32[4,32,512]{2,1,0:T(8,128)S(1)}, u32[]{:S(2)}, u32[]{:S(2)}) collective-permute-start(f32[4,32,512]{2,1,0:T(8,128)S(1)} %get-tuple-element.35), channel_id=1, source_target_pairs={{0,8},{8,0},{16,24},{24,16},{32,40},{40,32},{48,56},{56,48},{64,72... | collective-permute-start | bytes 786440 | tf_op jit(solution)/shard_map/ppermute | solution.py:488
  90.4 5.6 %collective-permute-start.8 = (f32[32,512]{1,0:T(8,128)S(1)}, f32[32,512]{1,0:T(8,128)S(1)}, u32[]{:S(2)}, u32[]{:S(2)}) collective-permute-start(f32[32,512]{1,0:T(8,128)S(1)} %get-tuple-element.37), channel_id=1, source_target_pairs={{0,32},{8,40},{16,48},{24,56},{32,0},{40,8},{48,16},{56,24},{64,96... | collective-permute-start | bytes 196616 | tf_op jit(solution)/shard_map/ppermute | solution.py:488
  93.1 5.8 %collective-permute-start.9 = (f32[32,512]{1,0:T(8,128)S(1)}, f32[32,512]{1,0:T(8,128)S(1)}, u32[]{:S(2)}, u32[]{:S(2)}) collective-permute-start(f32[32,512]{1,0:T(8,128)S(1)} %get-tuple-element.38), channel_id=1, source_target_pairs={{0,64},{8,72},{16,80},{24,88},{32,96},{40,104},{48,112},{56,120},{... | collective-permute-start | bytes 196616 | tf_op jit(solution)/shard_map/ppermute | solution.py:488
  93.1 6.5 %collective-permute-start.10 = (f32[32,512]{1,0:T(8,128)S(1)}, f32[32,512]{1,0:T(8,128)S(1)}, u32[]{:S(2)}, u32[]{:S(2)}) collective-permute-start(f32[32,512]{1,0:T(8,128)S(1)} %get-tuple-element.39), channel_id=1, source_target_pairs={{0,96},{8,104},{16,112},{24,120},{32,64},{40,72},{48,80},{56,88},{... | collective-permute-start | bytes 196616 | tf_op jit(solution)/shard_map/ppermute | solution.py:488
  100.2 7.6 %collective-permute-start.11 = (f32[8,512]{1,0:T(8,128)S(1)}, f32[8,512]{1,0:T(8,128)S(1)}, u32[]{:S(2)}, u32[]{:S(2)}) collective-permute-start(f32[8,512]{1,0:T(8,128)S(1)} %get-tuple-element.41), channel_id=1, source_target_pairs={{0,2},{1,3},{2,0},{3,1},{4,6},{5,7},{6,4},{7,5},{8,10},{9,11},{10,... | collective-permute-start | bytes 49160 | tf_op jit(solution)/shard_map/ppermute | solution.py:488
  101.1 6.6 %collective-permute-start.12 = (f32[8,512]{1,0:T(8,128)S(1)}, f32[8,512]{1,0:T(8,128)S(1)}, u32[]{:S(2)}, u32[]{:S(2)}) collective-permute-start(f32[8,512]{1,0:T(8,128)S(1)} %get-tuple-element.42), channel_id=1, source_target_pairs={{0,4},{1,5},{2,6},{3,7},{4,0},{5,1},{6,2},{7,3},{8,12},{9,13},{10,... | collective-permute-start | bytes 49160 | tf_op jit(solution)/shard_map/ppermute | solution.py:488
  103.7 5.9 %collective-permute-start.13 = (f32[8,512]{1,0:T(8,128)S(1)}, f32[8,512]{1,0:T(8,128)S(1)}, u32[]{:S(2)}, u32[]{:S(2)}) collective-permute-start(f32[8,512]{1,0:T(8,128)S(1)} %get-tuple-element.43), channel_id=1, source_target_pairs={{0,6},{1,7},{2,4},{3,5},{4,2},{5,3},{6,0},{7,1},{8,14},{9,15},{10,... | collective-permute-start | bytes 49160 | tf_op jit(solution)/shard_map/ppermute | solution.py:488
